TPU v7x, 512 devices: a whole 4x4x16 slice. The times are simulated.
512 devices in a mesh: pipe: 16 (over z), blk: 32 (over x, y, core).
Axes of the slice: x: 4, y: 4, z: 16, core: 2. Of those that a mesh axis runs over, the one named last changes fastest.
Arguments:
- stream: bfloat16 [16, 128, 6144], P('pipe', 'blk'), may hold values from -6 to 6
- arrivals: bfloat16 [3, 128, 6144], P(None, 'blk'), may hold values from -6 to 6
- ln_gain: bfloat16 [16, 6144], P('pipe'), may hold values from 0.099609375 to 1.8984375
- ln_bias: bfloat16 [16, 6144], P('pipe'), may hold values from -3 to 3
- up_weight: bfloat16 [16, 6144, 4096], P('pipe', None, 'blk'), may hold values from -0.078125 to 0.078125
- up_bias: bfloat16 [16, 4096], P('pipe', 'blk'), may hold values from -3 to 3
- down_weight: bfloat16 [16, 4096, 6144], P('pipe', 'blk'), may hold values from -0.1875 to 0.1875
- down_bias: bfloat16 [16, 6144], P('pipe'), may hold values from -3 to 3
- active: int32 [4, 16, 2, 16], P(None, 'pipe'), may hold values from -1 to 31, as said below
Outputs:
- passed: bfloat16 [16, 4, 128, 6144], P('pipe', None, 'blk')
Inputs may be any that keep to these rules, and one draw needn't show every extreme that they name: Each list holds between 8 and 16 distinct block ids, followed by -1 padding; some blocks are active far more often than others.
All inputs are finite; a program needn't handle non-finite values.
Results may differ from a plain program's by a relative error of at most 0.019.
Values may be sent and summed in bfloat16 or wider, within the bound.
No kernel may reach another device: no remote copies, remote signals or barrier semaphores. Data moves between devices by JAX's collectives and lax.ppermute only.
A program may use at most 64 MiB of HBM per device.

v0:
```python
import jax
import jax.numpy as jnp
from jax import lax
from jax.sharding import PartitionSpec as P

TILE = 64
TICKS = 4


def shifted(block, axis, distance):
    devices = range(lax.axis_size(axis))
    route = [(i - distance, i) for i in devices if i - distance in devices]
    return lax.ppermute(block, axis, route)


def layer_norm(rows, gain_row, shift_row):
    widened = rows.astype(jnp.float32)
    row_mean = jnp.mean(widened, axis=-1, keepdims=True)
    centred = widened - row_mean
    row_var = jnp.mean(centred * centred, axis=-1, keepdims=True)
    scaled = centred * lax.rsqrt(row_var + 1e-05)
    return (scaled * gain_row + shift_row).astype(jnp.bfloat16)


def on_device(
    stream, arrivals, ln_gain, ln_bias, up_weight, up_bias, down_weight, down_bias, active
):
    blocks = lax.axis_size("blk")
    my_index = lax.axis_index("blk")
    section = lax.axis_index("pipe")
    rows_dev = stream.shape[1]
    width = stream.shape[2]
    w_up = up_weight[0]
    b_up = up_bias[0].astype(jnp.float32)
    w_down = down_weight[0]
    gain_row = ln_gain[0].astype(jnp.float32)
    shift_row = ln_bias[0].astype(jnp.float32)
    b_down = down_bias[0].astype(jnp.float32)
    current = stream[0]
    results = []
    for step_index in range(TICKS):
        tile_lists = active[step_index, 0]
        tile_count = tile_lists.shape[0]
        owned_tiles = jnp.any(tile_lists == my_index, axis=1).astype(jnp.float32)
        normed = layer_norm(current, gain_row, shift_row)
        piece = lax.all_gather(normed, "blk", axis=0, tiled=True)
        row_index = jnp.arange(piece.shape[0], dtype=jnp.int32)
        matches = row_index[:, None] // TILE == jnp.arange(tile_count, dtype=jnp.int32)[None, :]
        row_flag = jnp.sum(matches.astype(jnp.float32) * owned_tiles[None, :], axis=1)
        preact = jnp.dot(piece, w_up, preferred_element_type=jnp.float32) + b_up
        activity = (jnp.maximum(preact, 0.0) * row_flag[:, None]).astype(jnp.bfloat16)
        partials = jnp.dot(activity, w_down, preferred_element_type=jnp.float32).astype(
            jnp.bfloat16
        )
        stacked = partials.reshape(blocks, rows_dev, width)
        received = lax.all_to_all(stacked, "blk", split_axis=0, concat_axis=0, tiled=True)
        summed = jnp.sum(received.astype(jnp.float32), axis=0)
        produced = (current.astype(jnp.float32) + summed + b_down).astype(jnp.bfloat16)
        results.append(produced)
        if step_index + 1 < TICKS:
            moved = shifted(produced, "pipe", 1)
            current = jnp.where(section == 0, arrivals[step_index], moved)
    return jnp.stack(results)[None]


def solution(mesh):
    return jax.shard_map(
        on_device,
        mesh=mesh,
        in_specs=(
            P("pipe", "blk", None),
            P(None, "blk", None),
            P("pipe", None),
            P("pipe", None),
            P("pipe", None, "blk"),
            P("pipe", "blk"),
            P("pipe", "blk", None),
            P("pipe", None),
            P(None, "pipe", None, None),
        ),
        out_specs=P("pipe", None, "blk", None),
        check_vma=False,
    )
```

profile of v0, /device:TPU:1, one launch (start us, length us, event | category | flops | bytes accessed | tf_op | source)
XLA Modules:
  0.0 441.8 jit_solution(18012084157302393708)
XLA Ops:
  6.5 1.1 convert_reduce_fusion.7
  7.6 1.0 fusion.90
  8.7 0.8 mul.174
  9.4 0.8 add.182
  10.2 1.5 fusion.105
  11.8 0.9 compare_reduce_fusion
  12.8 0.7 bitcast_convert_fusion
  13.4 62.7 %all-gather.9.cloned.1.call-done = bf16[32,4,6144]{2,1,0:T(4,128)(2,1)} async-done(((bf16[1,4,6144]{2,1,0:T(4,128)(2,1)}), bf16[32,4,6144]{2,1,0:T(4,128)(2,1)}) %all-gather.9.cloned.1.call-update) | async-done | bytes 1572880 | tf_op jit(solution)/shard_map/all_gather | solution.py:46
  76.2 3.7 reshape.139
  79.9 3.6 convolution_convert_fusion.3
  83.5 3.8 reshape.130
  87.3 5.4 %all-to-all-start = ((bf16[32,4,6144]{2,1,0:T(4,128)(2,1)}), bf16[32,4,6144]{2,1,0:T(4,128)(2,1)}, u32[]{:S(2)}, u32[]{:S(2)}) async-start(bf16[32,4,6144]{2,1,0:T(4,128)(2,1)} %reshape.130), calls=%async_computation | async-start | bytes 3145728 | tf_op jit(solution)/shard_map/all_to_all | solution.py:56
  92.8 22.6 %all-to-all-done = bf16[32,4,6144]{2,1,0:T(4,128)(2,1)} async-done(((bf16[32,4,6144]{2,1,0:T(4,128)(2,1)}), bf16[32,4,6144]{2,1,0:T(4,128)(2,1)}, u32[]{:S(2)}, u32[]{:S(2)}) %all-to-all-start) | async-done | bytes 1572896 | tf_op jit(solution)/shard_map/all_to_all | solution.py:56
  115.4 2.1 convert_reduce_fusion.3
  117.6 3.2 collective-permute-start
  120.8 1.2 collective-permute-done
  121.9 1.0 convert_reduce_fusion.6
  122.9 0.2 fusion.86
  123.1 0.7 fusion.106
  123.9 59.6 %all-gather.11.cloned.1.call-done = bf16[32,4,6144]{2,1,0:T(4,128)(2,1)} async-done(((bf16[1,4,6144]{2,1,0:T(4,128)(2,1)}), bf16[32,4,6144]{2,1,0:T(4,128)(2,1)}) %all-gather.11.cloned.1.call-update) | async-done | bytes 1572880 | tf_op jit(solution)/shard_map/all_gather | solution.py:46
  183.5 3.7 reshape.141
  187.2 3.6 convolution_convert_fusion.2
  190.8 3.8 reshape.131
  194.6 28.1 %all_to_all.20 = bf16[32,4,6144]{2,1,0:T(4,128)(2,1)S(1)} all-to-all(bf16[32,4,6144]{2,1,0:T(4,128)(2,1)} %reshape.131), channel_id=1, replica_groups=mesh['pipe'=16,'blk'=32] {'blk'}, dimensions={0} | all-to-all | bytes 3145728 | tf_op jit(solution)/shard_map/all_to_all | solution.py:56
  222.7 0.6 convert_reduce_fusion.2
  223.4 3.2 collective-permute-start.1
  226.6 1.3 collective-permute-done.1
  227.9 1.0 convert_reduce_fusion.5
  228.8 0.2 fusion.82
  229.1 0.7 fusion.107
  229.9 59.2 %all-gather.13.cloned.1.call-done = bf16[32,4,6144]{2,1,0:T(4,128)(2,1)} async-done(((bf16[1,4,6144]{2,1,0:T(4,128)(2,1)}), bf16[32,4,6144]{2,1,0:T(4,128)(2,1)}) %all-gather.13.cloned.1.call-update) | async-done | bytes 1572880 | tf_op jit(solution)/shard_map/all_gather | solution.py:46
  289.1 3.7 reshape.143
  292.8 3.6 convolution_convert_fusion.1
  296.4 3.8 reshape.132
  300.2 28.1 %all_to_all.21 = bf16[32,4,6144]{2,1,0:T(4,128)(2,1)S(1)} all-to-all(bf16[32,4,6144]{2,1,0:T(4,128)(2,1)} %reshape.132), channel_id=1, replica_groups=mesh['pipe'=16,'blk'=32] {'blk'}, dimensions={0} | all-to-all | bytes 3145728 | tf_op jit(solution)/shard_map/all_to_all | solution.py:56
  328.3 0.6 convert_reduce_fusion.1
  329.0 3.2 collective-permute-start.2
  332.1 1.3 collective-permute-done.2
  333.5 1.0 convert_reduce_fusion.4
  334.7 0.7 fusion.108
  335.4 59.3 %all-gather.15.cloned.1.call-done = bf16[32,4,6144]{2,1,0:T(4,128)(2,1)} async-done(((bf16[1,4,6144]{2,1,0:T(4,128)(2,1)}), bf16[32,4,6144]{2,1,0:T(4,128)(2,1)}) %all-gather.15.cloned.1.call-update) | async-done | bytes 1572880 | tf_op jit(solution)/shard_map/all_gather | solution.py:46
  394.7 3.7 reshape.145
  398.4 3.6 convolution_convert_fusion
  402.0 3.8 reshape.133
  405.8 5.2 %all-to-all-start.3 = ((bf16[32,4,6144]{2,1,0:T(4,128)(2,1)}), bf16[32,4,6144]{2,1,0:T(4,128)(2,1)S(1)}, u32[]{:S(2)}, u32[]{:S(2)}) async-start(bf16[32,4,6144]{2,1,0:T(4,128)(2,1)} %reshape.133), calls=%async_computation.3 | async-start | bytes 3145728 | tf_op jit(solution)/shard_map/all_to_all | solution.py:56
  411.1 22.6 %all-to-all-done.3 = bf16[32,4,6144]{2,1,0:T(4,128)(2,1)S(1)} async-done(((bf16[32,4,6144]{2,1,0:T(4,128)(2,1)}), bf16[32,4,6144]{2,1,0:T(4,128)(2,1)S(1)}, u32[]{:S(2)}, u32[]{:S(2)}) %all-to-all-start.3) | async-done | bytes 1572896 | tf_op jit(solution)/shard_map/all_to_all | solution.py:56
  433.7 0.6 convert_reduce_fusion
  434.4 0.9 maximum_bitcast_fusion
  (37 shorter events, 0.8 us)
Async XLA Ops:
  6.5 73.3 %copy-start = (bf16[1,128,6144]{2,1,0:T(8,128)(2,1)S(1)}, bf16[1,128,6144]{2,1,0:T(8,128)(2,1)}, u32[]{:S(2)}) copy-start(bf16[1,128,6144]{2,1,0:T(8,128)(2,1)} %param.15) | copy-start | bytes 4718596
  6.5 69.7 %all-gather.9.cloned.1.call-start = ((), (), s32[]{:S(2)}) async-start(), calls=%async_computation.4 | async-start | bytes 1622016 | tf_op jit(solution)/shard_map/all_gather | solution.py:46
  13.4 66.4 %copy-start.1 = (bf16[1,6144,128]{2,1,0:T(8,128)(2,1)S(1)}, bf16[1,6144,128]{2,1,0:T(8,128)(2,1)}, u32[]{:S(2)}) copy-start(bf16[1,6144,128]{2,1,0:T(8,128)(2,1)} %param.13) | copy-start | bytes 4718596
  87.3 5.5 %copy-start.3 = (bf16[1,6144]{1,0:T(2,128)(2,1)S(1)}, bf16[1,6144]{1,0:T(2,128)(2,1)}, u32[]{:S(2)}) copy-start(bf16[1,6144]{1,0:T(2,128)(2,1)} %param.16) | copy-start | bytes 36868
  87.3 28.1 %all-to-all-start = ((bf16[32,4,6144]{2,1,0:T(4,128)(2,1)}), bf16[32,4,6144]{2,1,0:T(4,128)(2,1)}, u32[]{:S(2)}, u32[]{:S(2)}) async-start(bf16[32,4,6144]{2,1,0:T(4,128)(2,1)} %reshape.130), calls=%async_computation | async-start | bytes 3145728 | tf_op jit(solution)/shard_map/all_to_all | solution.py:56
  92.7 24.8 %copy-start.2 = (bf16[1,4,6144]{2,1,0:T(4,128)(2,1)S(1)}, bf16[1,4,6144]{2,1,0:T(4,128)(2,1)}, u32[]{:S(2)}) copy-start(bf16[1,4,6144]{2,1,0:T(4,128)(2,1)} %param.9) | copy-start | bytes 147460
  92.7 90.8 %all-gather.11.cloned.1.call-start = ((), (), s32[]{:S(2)}) async-start(), calls=%async_computation.5 | async-start | bytes 1622016 | tf_op jit(solution)/shard_map/all_gather | solution.py:46
  117.6 4.3 collective-permute-start
  123.9 165.2 %all-gather.13.cloned.1.call-start = ((), (), s32[]{:S(2)}) async-start(), calls=%async_computation.6 | async-start | bytes 1622016 | tf_op jit(solution)/shard_map/all_gather | solution.py:46
  223.4 4.5 %collective-permute-start.1 = (bf16[4,6144]{1,0:T(4,128)(2,1)S(1)}, bf16[4,6144]{1,0:T(4,128)(2,1)S(1)}, u32[]{:S(2)}, u32[]{:S(2)}) collective-permute-start(bf16[4,6144]{1,0:T(4,128)(2,1)S(1)} %fusion.99), channel_id=1, source_target_pairs={{0,32},{32,64},{64,96},{96,128},{128,160},{160,192},{192,224},{224... | collective-permute-start | bytes 147464 | tf_op jit(solution)/shard_map/ppermute | solution.py:13
  229.9 164.8 %all-gather.15.cloned.1.call-start = ((), (), s32[]{:S(2)}) async-start(), calls=%async_computation.7 | async-start | bytes 1622016 | tf_op jit(solution)/shard_map/all_gather | solution.py:46
  329.0 4.5 %collective-permute-start.2 = (bf16[4,6144]{1,0:T(4,128)(2,1)S(1)}, bf16[4,6144]{1,0:T(4,128)(2,1)S(1)}, u32[]{:S(2)}, u32[]{:S(2)}) collective-permute-start(bf16[4,6144]{1,0:T(4,128)(2,1)S(1)} %fusion.101), channel_id=1, source_target_pairs={{0,32},{32,64},{64,96},{96,128},{128,160},{160,192},{192,224},{224... | collective-permute-start | bytes 147464 | tf_op jit(solution)/shard_map/ppermute | solution.py:13
  405.8 27.9 %all-to-all-start.3 = ((bf16[32,4,6144]{2,1,0:T(4,128)(2,1)}), bf16[32,4,6144]{2,1,0:T(4,128)(2,1)S(1)}, u32[]{:S(2)}, u32[]{:S(2)}) async-start(bf16[32,4,6144]{2,1,0:T(4,128)(2,1)} %reshape.133), calls=%async_computation.3 | async-start | bytes 3145728 | tf_op jit(solution)/shard_map/all_to_all | solution.py:56
Sparse Core Ops, SparseCore 0:
  11.9 64.2 all-gather.8
  124.0 59.4 all-gather.10
  230.0 59.0 all-gather.12
  335.6 59.0 all-gather.14
where the time goes:
time: 443 us; the launch traced here: 442 us
  waiting for transfers between devices  290 us (65%)
  blocking collectives  56.1 us (13%)
  local copies, waits for them, and re-layouts  29.9 us (7%)
  starting transfers between devices  20.3 us (5%)
  other arithmetic  17.7 us (4%)
  matrix products  14.5 us (3%)
  between operations  13.3 us (3%)
    all_gather x4, waiting for transfers between devices, on_device(): piece = lax.all_gather(normed, 'blk', axis=0, tiled=True)  241 us
    all_to_all x2, blocking collectives, on_device(): lax.all_to_all(stacked, 'blk', split_axis=0, concat_axis=0, tiled=True)  56.1 us
    all_to_all x2, waiting for transfers between devices, on_device(): lax.all_to_all(stacked, 'blk', split_axis=0, concat_axis=0, tiled=True)  45.3 us
    reshape x4, local copies, waits for them, and re-layouts, on_device(): stacked = partials.reshape(blocks, rows_dev, width)  15.2 us
    unnamed x12, local copies, waits for them, and re-layouts  14.7 us
    dot_general x4, matrix products, on_device(): jnp.dot(activity, w_down, preferred_element_type=jnp.float32)  14.5 us
    all_to_all x2, starting transfers between devices, on_device(): lax.all_to_all(stacked, 'blk', split_axis=0, concat_axis=0, tiled=True)  10.6 us
    ppermute x3, starting transfers between devices, shifted(): return lax.ppermute(block, axis, route)  9.54 us
  transfers between devices with their start and end apart: 9, of which 9 were waited for; matrix products, arithmetic and copies ran while one was open for 0% of the time, Pallas kernels for 0%

commit v1 on v0

v1 whole, which is shorter than its diff:
```python
import functools

import jax
import jax.numpy as jnp
from jax import lax
from jax.experimental import pallas as pl
from jax.experimental.pallas import tpu as pltpu
from jax.sharding import PartitionSpec as P

F32, BF16 = jnp.float32, jnp.bfloat16
TILE = 64
TICKS = 4
CHIPS = 16
EPS = 1e-05
SIDE = 128

VMEM = pl.BlockSpec(memory_space=pltpu.VMEM)
SMEM = pl.BlockSpec(memory_space=pltpu.SMEM)
PARAMS = pltpu.CompilerParams(vmem_limit_bytes=40 * 1024 * 1024)


def half_of(c, half):
    return pl.ds(pl.multiple_of(c * half, 128), half)


def split_kernel(stream_ref, arrivals_ref, keep_ref, send_ref):
    c = lax.axis_index("blk") % 2
    half = keep_ref.shape[2]
    keep_ref[0] = stream_ref[0, :, half_of(c, half)]
    send_ref[0] = stream_ref[0, :, half_of(1 - c, half)]
    keep_ref[1:] = arrivals_ref[:, :, half_of(c, half)]
    send_ref[1:] = arrivals_ref[:, :, half_of(1 - c, half)]


def weights_kernel(up_ref, up_far_ref, down_ref, down_far_ref, gain_ref, bias_ref, up_bias_ref, up_out, down_out, rows_out):
    c = lax.axis_index("blk") % 2
    half = up_far_ref.shape[0]
    block = up_far_ref.shape[1]
    up_out[:, :block] = up_ref[0, pl.ds(pl.multiple_of(c * half, 128), half), :]
    up_out[:, block:] = up_far_ref[...]
    down_out[:block] = down_ref[0, :, half_of(c, half)]
    down_out[block:] = down_far_ref[...]
    gain = gain_ref[:, half_of(c, half)].astype(F32)
    bias = bias_ref[:, half_of(c, half)].astype(F32)
    row = lax.broadcasted_iota(jnp.int32, (8, half), 0)
    both = jnp.where(row == 0, gain, jnp.where(row == 1, bias, 0.0)).astype(BF16)
    sums = jnp.dot(both, up_out[...], preferred_element_type=F32)
    row = lax.broadcasted_iota(jnp.int32, (8, block), 0)
    own = jnp.where(row == 1, up_bias_ref[...].astype(F32), 0.0)
    rows_out[:, :block] = sums[:, :block] + own
    rows_out[:, block:] = sums[:, block:]


def norm_kernel(step, moved_ref, keep_ref, far_ref, gain_ref, rows_out, send_out, scratch):
    c = lax.axis_index("blk") % 2
    half = rows_out.shape[1]

    def local():
        near, far = keep_ref[step].astype(F32), far_ref[step].astype(F32)

        @pl.when(c == 0)
        def _():
            scratch[0:4] = near
            scratch[4:8] = far

        @pl.when(c == 1)
        def _():
            scratch[0:4] = far
            scratch[4:8] = near

    if step == 0:
        local()
    else:
        first = lax.axis_index("pipe") == 0
        pl.when(first)(local)

        @pl.when(jnp.logical_not(first))
        def _():
            scratch[...] = moved_ref[...].astype(F32)

    rows = scratch[...]
    rows_out[...] = rows.astype(BF16)
    mean = jnp.mean(rows, axis=1, keepdims=True)
    centred = rows - mean
    square = jnp.sum(centred * centred, axis=1, keepdims=True)
    scaled = (centred * gain_ref[:, half_of(c, half)].astype(F32)).astype(BF16)
    lane = lax.broadcasted_iota(jnp.int32, (8, SIDE), 1)
    side = jnp.zeros((8, SIDE), F32)
    for base, value in ((0, mean), (3, square)):
        for piece in range(3):
            part = value.astype(BF16).astype(F32)
            side = jnp.where(lane == base + piece, part, side)
            value = value - part
    side = side.astype(BF16)
    for chip in range(send_out.shape[0]):
        send_out[chip, :, :half] = scaled
        send_out[chip, :, half:] = side


def up_kernel(gathered_ref, up_ref, rows_ref, out_ref):
    half, wide = up_ref.shape
    count = gathered_ref.shape[0]
    out_ref[:count, :wide] = jnp.dot(gathered_ref[:, :half], up_ref[...], preferred_element_type=F32)
    out_ref[:count, wide:] = gathered_ref[:, half:].astype(F32)
    out_ref[count:, :wide] = rows_ref[...]
    out_ref[count:, wide:] = jnp.zeros((8, SIDE), F32)


def down_kernel(step, near_ref, far_ref, active_ref, down_ref, out_ref):
    wide, half = down_ref.shape
    block = wide // 2
    count = out_ref.shape[0]
    j = lax.axis_index("blk")
    near_side, far_side = near_ref[:count, wide:], far_ref[:count, wide:]
    lane = lax.broadcasted_iota(jnp.int32, (count, SIDE), 1)
    apart = jnp.sum(jnp.where(lane < 3, near_side - far_side, 0.0), axis=1, keepdims=True) * 0.5
    square = jnp.sum(jnp.where((lane >= 3) & (lane < 6), near_side + far_side, 0.0), axis=1, keepdims=True)
    scale = lax.rsqrt(square / (2 * half) + apart * apart + EPS)
    tile = lax.broadcasted_iota(jnp.int32, (count, block), 0) // TILE
    acts = []
    for mine, other, owner in (((0, block), (block, wide), j), ((block, wide), (0, block), j + 1 - 2 * (j % 2))):
        near = near_ref[:count, mine[0] : mine[1]]
        far = far_ref[:count, other[0] : other[1]]
        gain_sum = near_ref[count : count + 1, mine[0] : mine[1]] - far_ref[count : count + 1, other[0] : other[1]]
        bias_sum = near_ref[count + 1 : count + 2, mine[0] : mine[1]] + far_ref[count + 1 : count + 2, other[0] : other[1]]
        flag = jnp.zeros((count, block), F32)
        for t in range(active_ref.shape[2]):
            found = jnp.int32(0)
            for k in range(active_ref.shape[3]):
                found = found | (active_ref[step, 0, t, k] == owner).astype(jnp.int32)
            flag = jnp.where(tile == t, found.astype(F32), flag)
        preact = scale * (near + far + apart * gain_sum) + bias_sum
        acts.append((jnp.maximum(preact, 0.0) * flag).astype(BF16))
    acts = jnp.concatenate(acts, axis=1)
    chunk = 512
    for at in range(0, half, chunk):
        out_ref[:, at : at + chunk] = jnp.dot(acts, down_ref[:, at : at + chunk], preferred_element_type=F32).astype(BF16)


def sum_kernel(parts_ref, rows_ref, bias_ref, out_ref):
    c = lax.axis_index("blk") % 2
    half = out_ref.shape[1]
    total = rows_ref[...].astype(F32) + bias_ref[:, half_of(c, half)].astype(F32)
    for chip in range(parts_ref.shape[0]):
        total += parts_ref[chip].astype(F32)
    out_ref[...] = total.astype(BF16)


def final_kernel(produced_refs, far_ref, out_ref):
    c = lax.axis_index("blk") % 2
    half = far_ref.shape[2]

    def at(core):
        for step, ref in enumerate(produced_refs):
            rows = ref[...].astype(F32)
            out_ref[0, step, :, core * half : (core + 1) * half] = rows[core * 4 : core * 4 + 4].astype(BF16)
        out_ref[0, :, :, (1 - core) * half : (2 - core) * half] = far_ref[...]

    pl.when(c == 0)(functools.partial(at, 0))
    pl.when(c == 1)(functools.partial(at, 1))


def gather_far_kernel(produced_refs, out_ref):
    c = lax.axis_index("blk") % 2

    def at(core):
        for step, ref in enumerate(produced_refs):
            rows = ref[...].astype(F32)
            out_ref[step] = rows[(1 - core) * 4 : (1 - core) * 4 + 4].astype(BF16)

    pl.when(c == 0)(functools.partial(at, 0))
    pl.when(c == 1)(functools.partial(at, 1))


def call(kernel, outs, *args, specs=None, scratch=()):
    single = isinstance(outs, jax.ShapeDtypeStruct)
    return pl.pallas_call(
        kernel,
        out_shape=outs,
        in_specs=list(specs) if specs else [VMEM] * len(args),
        out_specs=VMEM if single else [VMEM] * len(outs),
        scratch_shapes=list(scratch),
        compiler_params=PARAMS,
    )(*args)


def on_device(stream, arrivals, ln_gain, ln_bias, up_weight, up_bias, down_weight, down_bias, active):
    shape = jax.ShapeDtypeStruct
    blocks = lax.axis_size("blk")
    pipes = lax.axis_size("pipe")
    rows_dev, width = stream.shape[1], stream.shape[2]
    block = up_weight.shape[2]
    half = width // 2
    rows_chip = 2 * rows_dev
    rows_all = rows_chip * CHIPS
    c = lax.axis_index("blk") % 2
    same_core = [[2 * chip + core for chip in range(CHIPS)] for core in range(2)]

    def swap(x):
        return lax.ppermute(x, "blk", [(i, i ^ 1) for i in range(blocks)])

    def trade(x):
        return lax.all_to_all(x, "blk", 0, 0, axis_index_groups=same_core, tiled=True)

    keep, send = call(split_kernel, [shape((TICKS, rows_dev, half), BF16)] * 2, stream, arrivals)
    far = swap(send)
    up_far = swap(lax.dynamic_slice(up_weight[0], ((1 - c) * half, 0), (half, block)))
    down_far = swap(lax.dynamic_slice(down_weight[0], (0, (1 - c) * half), (block, half)))
    up_pair, down_pair, bias_rows = call(
        weights_kernel,
        [shape((half, 2 * block), BF16), shape((2 * block, half), BF16), shape((8, 2 * block), F32)],
        up_weight, up_far, down_weight, down_far, ln_gain, ln_bias, up_bias,
    )
    moved = None
    produced = []
    for step in range(TICKS):
        args = [keep, far, ln_gain] if step == 0 else [moved, keep, far, ln_gain]
        kernel = functools.partial(norm_kernel, step) if step else (lambda *refs: norm_kernel(0, None, *refs))
        rows, outgoing = call(
            kernel,
            [shape((rows_chip, half), BF16), shape((CHIPS, rows_chip, half + SIDE), BF16)],
            *args,
            scratch=[pltpu.VMEM((rows_chip, half), F32)],
        )
        gathered = trade(outgoing).reshape(rows_all, half + SIDE)
        near = call(up_kernel, shape((rows_all + 8, 2 * block + SIDE), F32), gathered, up_pair, bias_rows)
        partial = call(
            functools.partial(down_kernel, step),
            shape((rows_all, half), BF16),
            near, swap(near), active, down_pair,
            specs=[VMEM, VMEM, SMEM, VMEM],
        )
        received = trade(partial.reshape(CHIPS, rows_chip, half))
        done = call(sum_kernel, shape((rows_chip, half), BF16), received, rows, down_bias)
        produced.append(done)
        if step + 1 < TICKS:
            moved = lax.ppermute(done, "pipe", [(i, i + 1) for i in range(pipes - 1)])
    theirs = call(lambda *refs: gather_far_kernel(refs[:-1], refs[-1]), shape((TICKS, rows_dev, half), BF16), *produced)
    return call(
        lambda *refs: final_kernel(refs[:-2], refs[-2], refs[-1]),
        shape((1, TICKS, rows_dev, width), BF16),
        *produced, swap(theirs),
    )


def solution(mesh):
    return jax.shard_map(
        on_device,
        mesh=mesh,
        in_specs=(
            P("pipe", "blk", None),
            P(None, "blk", None),
            P("pipe", None),
            P("pipe", None),
            P("pipe", None, "blk"),
            P("pipe", "blk"),
            P("pipe", "blk", None),
            P("pipe", None),
            P(None, "pipe", None, None),
        ),
        out_specs=P("pipe", None, "blk", None),
        check_vma=False,
    )
```

time: 443 us -> 201 us (0.45)
  waiting for transfers between devices: 290 us -> 16.1 us
  blocking collectives: 56.1 us -> 110 us
  starting transfers between devices: 20.3 us -> 50.1 us
  local copies, waits for them, and re-layouts: 29.9 us -> 10 us
  other arithmetic: 17.7 us -> 0 us
  matrix products: 14.5 us -> 0 us
  between operations: 13.3 us -> 0.3 us
  Pallas kernels: 0 us -> 10.8 us
    all_gather x4 -> x0, waiting for transfers between devices: 241 us -> none  [on_device(): piece = lax.all_gather(normed, 'blk', axis=0, tiled=True)]
    all_to_all x2 -> x7, blocking collectives: 56.1 us -> 110 us  [trade(): lax.all_to_all(x, 'blk', 0, 0, axis_index_groups=same_core, tiled=True)]
    all_to_all x2 -> x1, waiting for transfers between devices: 45.3 us -> 7.41 us  [trade(): lax.all_to_all(x, 'blk', 0, 0, axis_index_groups=same_core, tiled=True)]
    ppermute x3 -> x11, starting transfers between devices: 9.54 us -> 45.8 us  [the longest x8 37.2 us: swap(): return lax.ppermute(x, 'blk', [(i, i ^ 1) for i in range(blocks)])]
    reshape x4 -> x0, local copies, waits for them, and re-layouts: 15.2 us -> none  [on_device(): stacked = partials.reshape(blocks, rows_dev, width)]
    dot_general x4 -> x0, matrix products: 14.5 us -> none  [on_device(): jnp.dot(activity, w_down, preferred_element_type=jnp.float32)]
    pallas_call x0 -> x20, Pallas kernels: none -> 10.8 us  [call(): pl.pallas_call(kernel, out_shape=outs, in_specs=list(specs) if specs else...]
    reduce_sum x13 -> x0, other arithmetic: 9.78 us -> none  [the longest x4 3.98 us: layer_norm(): row_mean = jnp.mean(widened, axis=-1, keepdims=True)]
  transfers between devices with their start and end apart: 9 -> 12, of which waited for: 9 -> 9; matrix products, arithmetic and copies ran while one was open for 0% -> 0% of each run, Pallas kernels for 0% -> 1%
where the time goes in v1:
time: 201 us; the launch traced here: 198 us
  blocking collectives  110 us (55%)
  starting transfers between devices  50.1 us (25%)
  waiting for transfers between devices  16.1 us (8%)
  Pallas kernels  10.8 us (5%)
  local copies, waits for them, and re-layouts  10 us (5%)
    all_to_all x7, blocking collectives, trade(): lax.all_to_all(x, 'blk', 0, 0, axis_index_groups=same_core, tiled=True)  110 us
    ppermute x8, starting transfers between devices, swap(): return lax.ppermute(x, 'blk', [(i, i ^ 1) for i in range(blocks)])  37.2 us
    pallas_call x20, Pallas kernels, call(): pl.pallas_call(kernel, out_shape=outs, in_specs=list(specs) if specs else...  10.8 us
    ppermute x3, starting transfers between devices, on_device(): moved = lax.ppermute(done, 'pipe', [(i, i + 1) for i in range(pipes - 1)])  8.59 us
    all_to_all x1, waiting for transfers between devices, trade(): lax.all_to_all(x, 'blk', 0, 0, axis_index_groups=same_core, tiled=True)  7.41 us
    unnamed x28, local copies, waits for them, and re-layouts  6.88 us
    ppermute x8, waiting for transfers between devices, swap(): return lax.ppermute(x, 'blk', [(i, i ^ 1) for i in range(blocks)])  5.19 us
    all_to_all x1, starting transfers between devices, trade(): lax.all_to_all(x, 'blk', 0, 0, axis_index_groups=same_core, tiled=True)  4.31 us
  transfers between devices with their start and end apart: 12, of which 9 were waited for; matrix products, arithmetic and copies ran while one was open for 0% of the time, Pallas kernels for 1%

profile of v1, /device:TPU:1, one launch (start us, length us, event | category | flops | bytes accessed | tf_op | source)
XLA Modules:
  0.0 197.7 jit_solution(10953742771604014247)
XLA Ops:
  0.0 2.2 %dynamic-slice_bitcast_fusion.1 = bf16[3072,128]{1,0:T(8,128)(2,1)} fusion(bf16[1,6144,128]{2,1,0:T(8,128)(2,1)} %up_ref.1, s32[]{:T(128)S(6)} %select_n.12), kind=kLoop, calls=%fused_computation.1 | loop fusion | bytes 1572868 | tf_op jit(solution)/shard_map/dynamic_slice | solution.py:207
  2.2 8.7 %collective-permute-start.1 = (bf16[3072,128]{1,0:T(8,128)(2,1)}, bf16[3072,128]{1,0:T(8,128)(2,1)S(1)}, u32[]{:S(2)}, u32[]{:S(2)}) collective-permute-start(bf16[3072,128]{1,0:T(8,128)(2,1)} %dynamic-slice_bitcast_fusion.1), channel_id=1, source_target_pairs={{0,1},{1,0},{2,3},{3,2},{4,5},{5,4},{6,7},{7,6},{8,9},{9,8},{10,11... | collective-permute-start | bytes 2359304 | tf_op jit(solution)/shard_map/ppermute | solution.py:200
  11.1 1.9 collective-permute-start
  13.0 1.0 dynamic-slice_bitcast_fusion
  14.0 2.4 %collective-permute-start.2 = (bf16[128,3072]{1,0:T(8,128)(2,1)}, bf16[128,3072]{1,0:T(8,128)(2,1)S(1)}, u32[]{:S(2)}, u32[]{:S(2)}) collective-permute-start(bf16[128,3072]{1,0:T(8,128)(2,1)} %dynamic-slice_bitcast_fusion), channel_id=1, source_target_pairs={{0,1},{1,0},{2,3},{3,2},{4,5},{5,4},{6,7},{7,6},{8,9},{9,8},{10,11... | collective-permute-start | bytes 2359304 | tf_op jit(solution)/shard_map/ppermute | solution.py:200
  16.4 1.2 shard_map.92
  17.6 4.3 %all-to-all-start = ((bf16[16,8,3200]{2,1,0:T(8,128)(2,1)}), bf16[16,8,3200]{2,1,0:T(8,128)(2,1)}, u32[]{:S(2)}, u32[]{:S(2)}) async-start(bf16[16,8,3200]{2,1,0:T(8,128)(2,1)} %get-tuple-element.20), calls=%async_computation | async-start | bytes 1638400 | tf_op jit(solution)/shard_map/all_to_all | solution.py:203
  21.9 0.9 copy-done.3
  22.8 0.9 copy-done.5
  23.7 1.4 copy-done
  25.1 1.4 copy-done.2
  26.5 1.1 copy-done.4
  27.6 1.1 copy-done.6
  28.8 0.7 shard_map.93
  29.4 7.4 %all-to-all-done = bf16[16,8,3200]{2,1,0:T(8,128)(2,1)} async-done(((bf16[16,8,3200]{2,1,0:T(8,128)(2,1)}), bf16[16,8,3200]{2,1,0:T(8,128)(2,1)}, u32[]{:S(2)}, u32[]{:S(2)}) %all-to-all-start) | async-done | bytes 819232 | tf_op jit(solution)/shard_map/all_to_all | solution.py:203
  36.8 1.5 shard_map.94.near_ref
  38.4 3.0 %collective-permute-start.3 = (f32[136,384]{1,0:T(8,128)S(1)}, f32[136,384]{1,0:T(8,128)S(1)}, u32[]{:S(2)}, u32[]{:S(2)}) collective-permute-start(f32[136,384]{1,0:T(8,128)S(1)} %shard_map.94.near_ref), channel_id=1, source_target_pairs={{0,1},{1,0},{2,3},{3,2},{4,5},{5,4},{6,7},{7,6},{8,9},{9,8},{10,11... | collective-permute-start | bytes 626696 | tf_op jit(solution)/shard_map/ppermute | solution.py:200
  41.4 1.1 collective-permute-done.3.far_ref
  42.5 1.0 shard_map.95
  43.5 16.2 %all_to_all.40.parts_ref = bf16[16,8,3072]{2,1,0:T(8,128)(2,1)S(1)} all-to-all(bf16[16,8,3072]{2,1,0:T(8,128)(2,1)S(1)} %bitcast.16), channel_id=1, replica_groups={{0,2,4,6,8,10,12,14,16,18,20,22,24,26,28,30},{1,3,5,7,9,11,13,15,17,19,..., dimensions={0} | all-to-all | bytes 1572864 | tf_op jit(solution)/shard_map/all_to_all | solution.py:203
  59.9 1.3 collective-permute-start.4
  61.2 1.2 collective-permute-done.4.moved_ref
  62.4 0.2 shard_map.97
  62.6 15.4 %all_to_all.41 = bf16[16,8,3200]{2,1,0:T(8,128)(2,1)S(1)} all-to-all(bf16[16,8,3200]{2,1,0:T(8,128)(2,1)S(1)} %get-tuple-element.25), channel_id=1, replica_groups={{0,2,4,6,8,10,12,14,16,18,20,22,24,26,28,30},{1,3,5,7,9,11,13,15,17,19,..., dimensions={0} | all-to-all | bytes 1638400 | tf_op jit(solution)/shard_map/all_to_all | solution.py:203
  78.1 0.4 shard_map.98.near_ref
  78.5 5.3 %collective-permute-start.5 = (f32[136,384]{1,0:T(8,128)S(1)}, f32[136,384]{1,0:T(8,128)S(1)}, u32[]{:S(2)}, u32[]{:S(2)}) collective-permute-start(f32[136,384]{1,0:T(8,128)S(1)} %shard_map.98.near_ref), channel_id=1, source_target_pairs={{0,1},{1,0},{2,3},{3,2},{4,5},{5,4},{6,7},{7,6},{8,9},{9,8},{10,11... | collective-permute-start | bytes 626696 | tf_op jit(solution)/shard_map/ppermute | solution.py:200
  83.8 1.1 collective-permute-done.5.far_ref
  84.8 1.0 shard_map.99
  85.9 16.5 %all_to_all.42.parts_ref = bf16[16,8,3072]{2,1,0:T(8,128)(2,1)S(1)} all-to-all(bf16[16,8,3072]{2,1,0:T(8,128)(2,1)S(1)} %bitcast.17), channel_id=1, replica_groups={{0,2,4,6,8,10,12,14,16,18,20,22,24,26,28,30},{1,3,5,7,9,11,13,15,17,19,..., dimensions={0} | all-to-all | bytes 1572864 | tf_op jit(solution)/shard_map/all_to_all | solution.py:203
  102.5 3.6 %collective-permute-start.6 = (bf16[8,3072]{1,0:T(8,128)(2,1)S(1)}, bf16[8,3072]{1,0:T(8,128)(2,1)S(1)}, u32[]{:S(2)}, u32[]{:S(2)}) collective-permute-start(bf16[8,3072]{1,0:T(8,128)(2,1)S(1)} %shard_map.100.refs_1_), channel_id=1, source_target_pairs={{0,32},{32,64},{64,96},{96,128},{128,160},{160,192},{192,224},{224... | collective-permute-start | bytes 147464 | tf_op jit(solution)/shard_map/ppermute | solution.py:237
  106.1 1.2 collective-permute-done.6.moved_ref
  107.5 14.6 %all_to_all.43 = bf16[16,8,3200]{2,1,0:T(8,128)(2,1)S(1)} all-to-all(bf16[16,8,3200]{2,1,0:T(8,128)(2,1)S(1)} %get-tuple-element.27), channel_id=1, replica_groups={{0,2,4,6,8,10,12,14,16,18,20,22,24,26,28,30},{1,3,5,7,9,11,13,15,17,19,..., dimensions={0} | all-to-all | bytes 1638400 | tf_op jit(solution)/shard_map/all_to_all | solution.py:203
  122.2 0.4 shard_map.102.near_ref
  122.6 6.1 %collective-permute-start.7 = (f32[136,384]{1,0:T(8,128)S(1)}, f32[136,384]{1,0:T(8,128)S(1)}, u32[]{:S(2)}, u32[]{:S(2)}) collective-permute-start(f32[136,384]{1,0:T(8,128)S(1)} %shard_map.102.near_ref), channel_id=1, source_target_pairs={{0,1},{1,0},{2,3},{3,2},{4,5},{5,4},{6,7},{7,6},{8,9},{9,8},{10,11... | collective-permute-start | bytes 626696 | tf_op jit(solution)/shard_map/ppermute | solution.py:200
  128.7 1.1 collective-permute-done.7.far_ref
  129.7 1.1 shard_map.103
  130.8 16.5 %all_to_all.44.parts_ref = bf16[16,8,3072]{2,1,0:T(8,128)(2,1)S(1)} all-to-all(bf16[16,8,3072]{2,1,0:T(8,128)(2,1)S(1)} %bitcast.18), channel_id=1, replica_groups={{0,2,4,6,8,10,12,14,16,18,20,22,24,26,28,30},{1,3,5,7,9,11,13,15,17,19,..., dimensions={0} | all-to-all | bytes 1572864 | tf_op jit(solution)/shard_map/all_to_all | solution.py:203
  147.4 3.7 %collective-permute-start.8 = (bf16[8,3072]{1,0:T(8,128)(2,1)S(1)}, bf16[8,3072]{1,0:T(8,128)(2,1)S(1)}, u32[]{:S(2)}, u32[]{:S(2)}) collective-permute-start(bf16[8,3072]{1,0:T(8,128)(2,1)S(1)} %shard_map.104.refs_2_), channel_id=1, source_target_pairs={{0,32},{32,64},{64,96},{96,128},{128,160},{160,192},{192,224},{224... | collective-permute-start | bytes 147464 | tf_op jit(solution)/shard_map/ppermute | solution.py:237
  151.1 1.2 collective-permute-done.8.moved_ref
  152.5 14.6 %all_to_all.45 = bf16[16,8,3200]{2,1,0:T(8,128)(2,1)S(1)} all-to-all(bf16[16,8,3200]{2,1,0:T(8,128)(2,1)S(1)} %get-tuple-element.29), channel_id=1, replica_groups={{0,2,4,6,8,10,12,14,16,18,20,22,24,26,28,30},{1,3,5,7,9,11,13,15,17,19,..., dimensions={0} | all-to-all | bytes 1638400 | tf_op jit(solution)/shard_map/all_to_all | solution.py:203
  167.1 0.4 shard_map.106.near_ref
  167.5 6.1 %collective-permute-start.9 = (f32[136,384]{1,0:T(8,128)S(1)}, f32[136,384]{1,0:T(8,128)S(1)}, u32[]{:S(2)}, u32[]{:S(2)}) collective-permute-start(f32[136,384]{1,0:T(8,128)S(1)} %shard_map.106.near_ref), channel_id=1, source_target_pairs={{0,1},{1,0},{2,3},{3,2},{4,5},{5,4},{6,7},{7,6},{8,9},{9,8},{10,11... | collective-permute-start | bytes 626696 | tf_op jit(solution)/shard_map/ppermute | solution.py:200
  173.6 1.1 collective-permute-done.9.far_ref
  174.6 1.0 shard_map.107
  175.7 16.5 %all_to_all.46.parts_ref = bf16[16,8,3072]{2,1,0:T(8,128)(2,1)S(1)} all-to-all(bf16[16,8,3072]{2,1,0:T(8,128)(2,1)S(1)} %bitcast.15), channel_id=1, replica_groups={{0,2,4,6,8,10,12,14,16,18,20,22,24,26,28,30},{1,3,5,7,9,11,13,15,17,19,..., dimensions={0} | all-to-all | bytes 1572864 | tf_op jit(solution)/shard_map/all_to_all | solution.py:203
  192.4 3.7 %collective-permute-start.10 = (bf16[4,4,3072]{2,1,0:T(4,128)(2,1)S(1)}, bf16[4,4,3072]{2,1,0:T(4,128)(2,1)S(1)}, u32[]{:S(2)}, u32[]{:S(2)}) collective-permute-start(bf16[4,4,3072]{2,1,0:T(4,128)(2,1)S(1)} %shard_map.109), channel_id=1, source_target_pairs={{0,1},{1,0},{2,3},{3,2},{4,5},{5,4},{6,7},{7,6},{8,9},{9,8},{10,11... | collective-permute-start | bytes 294920 | tf_op jit(solution)/shard_map/ppermute | solution.py:200
  196.1 0.9 collective-permute-done.10.refs_4_
  197.0 0.7 shard_map.110
  (33 shorter events, 1.1 us)
Async XLA Ops:
  0.0 11.0 %copy-start.9 = (bf16[3,4,6144]{2,1,0:T(4,128)(2,1)S(1)}, bf16[3,4,6144]{2,1,0:T(4,128)(2,1)}, u32[]{:S(2)}) copy-start(bf16[3,4,6144]{2,1,0:T(4,128)(2,1)} %arrivals_ref.1) | copy-start | bytes 442372
  0.0 11.0 %copy-start.11 = (bf16[1,4,6144]{2,1,0:T(4,128)(2,1)S(1)}, bf16[1,4,6144]{2,1,0:T(4,128)(2,1)}, u32[]{:S(2)}) copy-start(bf16[1,4,6144]{2,1,0:T(4,128)(2,1)} %stream_ref.1) | copy-start | bytes 147460
  0.0 13.0 %copy-start.1 = (bf16[1,128,6144]{2,1,0:T(8,128)(2,1)S(1)}, bf16[1,128,6144]{2,1,0:T(8,128)(2,1)}, u32[]{:S(2)}) copy-start(bf16[1,128,6144]{2,1,0:T(8,128)(2,1)} %down_ref.1) | copy-start | bytes 4718596
  0.0 16.4 %copy-start.7 = (bf16[1,6144]{1,0:T(2,128)(2,1)S(1)}, bf16[1,6144]{1,0:T(2,128)(2,1)}, u32[]{:S(2)}) copy-start(bf16[1,6144]{1,0:T(2,128)(2,1)} %gain_ref.7) | copy-start | bytes 36868
  2.2 19.7 %collective-permute-start.1 = (bf16[3072,128]{1,0:T(8,128)(2,1)}, bf16[3072,128]{1,0:T(8,128)(2,1)S(1)}, u32[]{:S(2)}, u32[]{:S(2)}) collective-permute-start(bf16[3072,128]{1,0:T(8,128)(2,1)} %dynamic-slice_bitcast_fusion.1), channel_id=1, source_target_pairs={{0,1},{1,0},{2,3},{3,2},{4,5},{5,4},{6,7},{7,6},{8,9},{9,8},{10,11... | collective-permute-start | bytes 2359304 | tf_op jit(solution)/shard_map/ppermute | solution.py:200
  11.0 12.6 %copy-start.12 = (bf16[1,6144]{1,0:T(2,128)(2,1)S(1)}, bf16[1,6144]{1,0:T(2,128)(2,1)}, u32[]{:S(2)}) copy-start(bf16[1,6144]{1,0:T(2,128)(2,1)} %bias_ref.5) | copy-start | bytes 36868
  11.1 12.6 %copy-start.13 = (bf16[1,128]{1,0:T(2,128)(2,1)S(1)}, bf16[1,128]{1,0:T(2,128)(2,1)}, u32[]{:S(2)}) copy-start(bf16[1,128]{1,0:T(2,128)(2,1)} %up_bias_ref.1) | copy-start | bytes 772
  11.1 5.3 %collective-permute-start = (bf16[4,4,3072]{2,1,0:T(4,128)(2,1)S(1)}, bf16[4,4,3072]{2,1,0:T(4,128)(2,1)S(1)}, u32[]{:S(2)}, u32[]{:S(2)}) collective-permute-start(bf16[4,4,3072]{2,1,0:T(4,128)(2,1)S(1)} %get-tuple-element.19), channel_id=1, source_target_pairs={{0,1},{1,0},{2,3},{3,2},{4,5},{5,4},{6,7},{7,6},{8,9},{9,8},{10,11... | collective-permute-start | bytes 294920 | tf_op jit(solution)/shard_map/ppermute | solution.py:200
  14.0 8.8 %collective-permute-start.2 = (bf16[128,3072]{1,0:T(8,128)(2,1)}, bf16[128,3072]{1,0:T(8,128)(2,1)S(1)}, u32[]{:S(2)}, u32[]{:S(2)}) collective-permute-start(bf16[128,3072]{1,0:T(8,128)(2,1)} %dynamic-slice_bitcast_fusion), channel_id=1, source_target_pairs={{0,1},{1,0},{2,3},{3,2},{4,5},{5,4},{6,7},{7,6},{8,9},{9,8},{10,11... | collective-permute-start | bytes 2359304 | tf_op jit(solution)/shard_map/ppermute | solution.py:200
  17.6 19.3 %all-to-all-start = ((bf16[16,8,3200]{2,1,0:T(8,128)(2,1)}), bf16[16,8,3200]{2,1,0:T(8,128)(2,1)}, u32[]{:S(2)}, u32[]{:S(2)}) async-start(bf16[16,8,3200]{2,1,0:T(8,128)(2,1)} %get-tuple-element.20), calls=%async_computation | async-start | bytes 1638400 | tf_op jit(solution)/shard_map/all_to_all | solution.py:203
  21.9 0.9 copy-start.3
  22.8 0.9 copy-start.5
  23.7 1.4 copy-start
  25.1 1.4 copy-start.2
  26.5 1.1 copy-start.4
  27.6 1.1 copy-start.6
  29.4 13.1 %copy-start.10 = (s32[4,1,2,16]{3,2,1,0:T(2,128)S(1)}, s32[4,1,2,16]{3,2,1,0:T(2,128)}, u32[]{:S(2)}) copy-start(s32[4,1,2,16]{3,2,1,0:T(2,128)} %active_ref.7) | copy-start | bytes 1540
  38.4 4.1 %collective-permute-start.3 = (f32[136,384]{1,0:T(8,128)S(1)}, f32[136,384]{1,0:T(8,128)S(1)}, u32[]{:S(2)}, u32[]{:S(2)}) collective-permute-start(f32[136,384]{1,0:T(8,128)S(1)} %shard_map.94.near_ref), channel_id=1, source_target_pairs={{0,1},{1,0},{2,3},{3,2},{4,5},{5,4},{6,7},{7,6},{8,9},{9,8},{10,11... | collective-permute-start | bytes 626696 | tf_op jit(solution)/shard_map/ppermute | solution.py:200
  42.5 17.3 %copy-start.8 = (bf16[1,6144]{1,0:T(2,128)(2,1)S(1)}, bf16[1,6144]{1,0:T(2,128)(2,1)}, u32[]{:S(2)}) copy-start(bf16[1,6144]{1,0:T(2,128)(2,1)} %bias_ref.9) | copy-start | bytes 36868
  59.9 2.5 %collective-permute-start.4 = (bf16[8,3072]{1,0:T(8,128)(2,1)S(1)}, bf16[8,3072]{1,0:T(8,128)(2,1)S(1)}, u32[]{:S(2)}, u32[]{:S(2)}) collective-permute-start(bf16[8,3072]{1,0:T(8,128)(2,1)S(1)} %shard_map.96.refs_0_), channel_id=1, source_target_pairs={{0,32},{32,64},{64,96},{96,128},{128,160},{160,192},{192,224},{224... | collective-permute-start | bytes 147464 | tf_op jit(solution)/shard_map/ppermute | solution.py:237
  78.5 6.3 %collective-permute-start.5 = (f32[136,384]{1,0:T(8,128)S(1)}, f32[136,384]{1,0:T(8,128)S(1)}, u32[]{:S(2)}, u32[]{:S(2)}) collective-permute-start(f32[136,384]{1,0:T(8,128)S(1)} %shard_map.98.near_ref), channel_id=1, source_target_pairs={{0,1},{1,0},{2,3},{3,2},{4,5},{5,4},{6,7},{7,6},{8,9},{9,8},{10,11... | collective-permute-start | bytes 626696 | tf_op jit(solution)/shard_map/ppermute | solution.py:200
  102.5 4.8 %collective-permute-start.6 = (bf16[8,3072]{1,0:T(8,128)(2,1)S(1)}, bf16[8,3072]{1,0:T(8,128)(2,1)S(1)}, u32[]{:S(2)}, u32[]{:S(2)}) collective-permute-start(bf16[8,3072]{1,0:T(8,128)(2,1)S(1)} %shard_map.100.refs_1_), channel_id=1, source_target_pairs={{0,32},{32,64},{64,96},{96,128},{128,160},{160,192},{192,224},{224... | collective-permute-start | bytes 147464 | tf_op jit(solution)/shard_map/ppermute | solution.py:237
  122.6 7.2 %collective-permute-start.7 = (f32[136,384]{1,0:T(8,128)S(1)}, f32[136,384]{1,0:T(8,128)S(1)}, u32[]{:S(2)}, u32[]{:S(2)}) collective-permute-start(f32[136,384]{1,0:T(8,128)S(1)} %shard_map.102.near_ref), channel_id=1, source_target_pairs={{0,1},{1,0},{2,3},{3,2},{4,5},{5,4},{6,7},{7,6},{8,9},{9,8},{10,11... | collective-permute-start | bytes 626696 | tf_op jit(solution)/shard_map/ppermute | solution.py:200
  147.4 4.8 %collective-permute-start.8 = (bf16[8,3072]{1,0:T(8,128)(2,1)S(1)}, bf16[8,3072]{1,0:T(8,128)(2,1)S(1)}, u32[]{:S(2)}, u32[]{:S(2)}) collective-permute-start(bf16[8,3072]{1,0:T(8,128)(2,1)S(1)} %shard_map.104.refs_2_), channel_id=1, source_target_pairs={{0,32},{32,64},{64,96},{96,128},{128,160},{160,192},{192,224},{224... | collective-permute-start | bytes 147464 | tf_op jit(solution)/shard_map/ppermute | solution.py:237
  167.5 7.1 %collective-permute-start.9 = (f32[136,384]{1,0:T(8,128)S(1)}, f32[136,384]{1,0:T(8,128)S(1)}, u32[]{:S(2)}, u32[]{:S(2)}) collective-permute-start(f32[136,384]{1,0:T(8,128)S(1)} %shard_map.106.near_ref), channel_id=1, source_target_pairs={{0,1},{1,0},{2,3},{3,2},{4,5},{5,4},{6,7},{7,6},{8,9},{9,8},{10,11... | collective-permute-start | bytes 626696 | tf_op jit(solution)/shard_map/ppermute | solution.py:200
  192.4 4.6 %collective-permute-start.10 = (bf16[4,4,3072]{2,1,0:T(4,128)(2,1)S(1)}, bf16[4,4,3072]{2,1,0:T(4,128)(2,1)S(1)}, u32[]{:S(2)}, u32[]{:S(2)}) collective-permute-start(bf16[4,4,3072]{2,1,0:T(4,128)(2,1)S(1)} %shard_map.109), channel_id=1, source_target_pairs={{0,1},{1,0},{2,3},{3,2},{4,5},{5,4},{6,7},{7,6},{8,9},{9,8},{10,11... | collective-permute-start | bytes 294920 | tf_op jit(solution)/shard_map/ppermute | solution.py:200

commit v2 on v0

v2 whole, which is shorter than its diff:
```python
import functools

import jax
import jax.numpy as jnp
from jax import lax
from jax.experimental import pallas as pl
from jax.experimental.pallas import tpu as pltpu
from jax.sharding import PartitionSpec as P

F32, BF16 = jnp.float32, jnp.bfloat16
TICKS = 4
CHIPS = 16
EPS = 1e-05

VMEM = pl.BlockSpec(memory_space=pltpu.VMEM)
SMEM = pl.BlockSpec(memory_space=pltpu.SMEM)
PARAMS = pltpu.CompilerParams(vmem_limit_bytes=40 * 1024 * 1024)


def is_first(shape):
    return lax.broadcasted_iota(jnp.int32, shape, 0) % 8 < 4


def halves(row_ref, half):
    row = row_ref[...].astype(F32)
    return jnp.where(is_first((8, half)), row[:, :half], row[:, half:])


def row_sum(x):
    part = jnp.broadcast_to(jnp.sum(x, axis=1, keepdims=True), (8, 128))
    return (part + pltpu.roll(part, 4, 0))[:, :1]


def arrange_kernel(stream_ref, arrivals_ref, out_ref, scratch):
    half = out_ref.shape[2]
    for item in range(TICKS):
        rows = (stream_ref[0] if item == 0 else arrivals_ref[item - 1]).astype(F32)
        scratch[item, 0:4] = rows[:, :half]
        scratch[item, 4:8] = rows[:, half:]
        out_ref[item] = scratch[item].astype(BF16)


def norm_kernel(step, moved_ref, local_ref, gain_ref, bias_ref, rows_out, send_out):
    half = rows_out.shape[1]
    rows = local_ref[step].astype(F32)
    if step:
        first = jnp.broadcast_to(lax.axis_index("pipe") == 0, rows.shape)
        rows = jnp.where(first, rows, moved_ref[...].astype(F32))
    rows_out[...] = rows.astype(BF16)
    centred = rows - row_sum(rows) * (0.5 / half)
    var = row_sum(centred * centred) * (0.5 / half)
    scaled = centred * lax.rsqrt(var + EPS)
    normed = (scaled * halves(gain_ref, half) + halves(bias_ref, half)).astype(BF16)
    for chip in range(CHIPS):
        send_out[chip] = normed


def ffn_kernel(step, rows_ref, up_near, up_far, bias_near, bias_far, active_ref, down_near, down_far, out_ref):
    count, half = rows_ref.shape
    block = up_near.shape[2]
    chunk = 512
    j = lax.axis_index("blk")
    tile = j % 2

    def up(at):
        return jnp.concatenate([up_near[0, at : at + chunk], up_far[0, at : at + chunk]], axis=1)

    def down(at):
        return jnp.concatenate([down_near[0, :, at : at + chunk], down_far[0, :, at : at + chunk]], axis=0)

    first = jnp.zeros((count, 2 * block), F32)
    second = jnp.zeros((count, 2 * block), F32)
    for at in range(0, half, chunk):
        rows = rows_ref[:, at : at + chunk]
        first += jnp.dot(rows, up(at), preferred_element_type=F32)
        second += jnp.dot(rows, up(half + at), preferred_element_type=F32)
    low = is_first(first.shape)
    own = jnp.where(low, first, second)
    preact = own + jnp.where(low, pltpu.roll(own, count - 4, 0), pltpu.roll(own, 4, 0))
    flags = []
    for owner in (j, j + 1 - 2 * tile):
        found = jnp.int32(0)
        for k in range(active_ref.shape[3]):
            found = found | (active_ref[step, 0, tile, k] == owner).astype(jnp.int32)
        flags.append(jnp.broadcast_to(found.astype(F32), (1, block)))
    flag = jnp.concatenate(flags, axis=1)
    bias = jnp.concatenate([bias_near[...], bias_far[...]], axis=1).astype(F32)
    acts = (jnp.maximum(preact + bias, 0.0) * flag).astype(BF16)
    low = is_first((count, chunk))
    for at in range(0, half, chunk):
        one = jnp.dot(acts, down(at), preferred_element_type=F32)
        two = jnp.dot(acts, down(half + at), preferred_element_type=F32)
        out_ref[:, at : at + chunk] = jnp.where(low, one, two).astype(BF16)


def sum_kernel(parts_ref, rows_ref, bias_ref, *refs):
    before, out_ref = refs[:-1], refs[-1]
    half = rows_ref.shape[1]
    total = rows_ref[...].astype(F32) + halves(bias_ref, half)
    for chip in range(CHIPS):
        total += parts_ref[chip].astype(F32)
    if before:
        for step, ref in enumerate(before):
            out_ref[step] = ref[...]
        out_ref[len(before)] = total.astype(BF16)
    else:
        out_ref[...] = total.astype(BF16)


def final_kernel(rows_ref, out_ref):
    half = rows_ref.shape[2]
    for step in range(TICKS):
        rows = rows_ref[step].astype(F32)
        out_ref[0, step, :, :half] = rows[0:4].astype(BF16)
        out_ref[0, step, :, half:] = rows[4:8].astype(BF16)


def call(kernel, outs, *args, specs=None, scratch=()):
    single = isinstance(outs, jax.ShapeDtypeStruct)
    return pl.pallas_call(
        kernel,
        out_shape=outs,
        in_specs=list(specs) if specs else [VMEM] * len(args),
        out_specs=VMEM if single else [VMEM] * len(outs),
        scratch_shapes=list(scratch),
        compiler_params=PARAMS,
    )(*args)


def on_device(stream, arrivals, ln_gain, ln_bias, up_weight, up_bias, down_weight, down_bias, active):
    shape = jax.ShapeDtypeStruct
    blocks = lax.axis_size("blk")
    pipes = lax.axis_size("pipe")
    rows_dev, width = stream.shape[1], stream.shape[2]
    half = width // 2
    rows_half = 2 * rows_dev
    same_core = [[2 * chip + core for chip in range(CHIPS)] for core in range(2)]
    homes = [(j, 2 * (j % CHIPS) + j // CHIPS) for j in range(blocks)]

    def swap(x):
        return lax.ppermute(x, "blk", [(i, i ^ 1) for i in range(blocks)])

    def trade(x):
        return lax.all_to_all(x, "blk", 0, 0, axis_index_groups=same_core, tiled=True)

    arranged = call(
        arrange_kernel,
        shape((TICKS, rows_half, half), BF16),
        stream, arrivals,
        scratch=[pltpu.VMEM((TICKS, rows_half, half), F32)],
    )
    local = lax.ppermute(arranged, "blk", homes)
    moved = None
    produced = []
    for step in range(TICKS):
        args = [local, ln_gain, ln_bias] if step == 0 else [moved, local, ln_gain, ln_bias]
        kernel = functools.partial(norm_kernel, step) if step else functools.partial(norm_kernel, 0, None)
        rows, outgoing = call(
            kernel,
            [shape((rows_half, half), BF16), shape((CHIPS, rows_half, half), BF16)],
            *args,
        )
        if step == 0:
            outgoing, *weights = lax.optimization_barrier((outgoing, up_weight, down_weight, up_bias))
            up_far, down_far, bias_far = map(swap, weights)
        gathered = trade(outgoing).reshape(CHIPS * rows_half, half)
        partial = call(
            functools.partial(ffn_kernel, step),
            shape((CHIPS * rows_half, half), BF16),
            gathered, up_weight, up_far, up_bias, bias_far, active, down_weight, down_far,
            specs=[VMEM] * 5 + [SMEM] + [VMEM] * 2,
        )
        received = trade(partial.reshape(CHIPS, rows_half, half))
        if step + 1 < TICKS:
            done = call(sum_kernel, shape((rows_half, half), BF16), received, rows, down_bias)
            produced.append(done)
            moved = lax.ppermute(done, "pipe", [(i, i + 1) for i in range(pipes - 1)])
        else:
            done = call(sum_kernel, shape((TICKS, rows_half, half), BF16), received, rows, down_bias, *produced)
    back = lax.ppermute(done, "blk", [(home, j) for j, home in homes])
    return call(final_kernel, shape((1, TICKS, rows_dev, width), BF16), back)


def solution(mesh):
    return jax.shard_map(
        on_device,
        mesh=mesh,
        in_specs=(
            P("pipe", "blk", None),
            P(None, "blk", None),
            P("pipe", None),
            P("pipe", None),
            P("pipe", None, "blk"),
            P("pipe", "blk"),
            P("pipe", "blk", None),
            P("pipe", None),
            P(None, "pipe", None, None),
        ),
        out_specs=P("pipe", None, "blk", None),
        check_vma=False,
    )
```

time: 443 us -> 194 us (0.44)
  the two profiles are of different devices: /device:TPU:1 before, /device:TPU:266 now
where the time goes in v2:
time: 194 us; the launch traced here: 193 us
  blocking collectives  107 us (55%)
  waiting for transfers between devices  38 us (20%)
  starting transfers between devices  28.4 us (15%)
  Pallas kernels  13.5 us (7%)
  local copies, waits for them, and re-layouts  5.62 us (3%)
    all_to_all x7, blocking collectives, trade(): lax.all_to_all(x, 'blk', 0, 0, axis_index_groups=same_core, tiled=True)  107 us
    ppermute x3, waiting for transfers between devices, on_device(): moved = lax.ppermute(done, 'pipe', [(i, i + 1) for i in range(pipes - 1)])  14.8 us
    pallas_call x14, Pallas kernels, call(): pl.pallas_call(kernel, out_shape=outs, in_specs=list(specs) if specs else...  13.5 us
    all_to_all x1, starting transfers between devices, trade(): lax.all_to_all(x, 'blk', 0, 0, axis_index_groups=same_core, tiled=True)  8.95 us
    ppermute x1, waiting for transfers between devices, on_device(): back = lax.ppermute(done, 'blk', [(home, j) for j, home in homes])  8.64 us
    all_to_all x1, waiting for transfers between devices, trade(): lax.all_to_all(x, 'blk', 0, 0, axis_index_groups=same_core, tiled=True)  8.31 us
    ppermute x3, starting transfers between devices, on_device(): moved = lax.ppermute(done, 'pipe', [(i, i + 1) for i in range(pipes - 1)])  6.9 us
    ppermute x3, starting transfers between devices, swap(): return lax.ppermute(x, 'blk', [(i, i ^ 1) for i in range(blocks)])  6.24 us
  transfers between devices with their start and end apart: 9, of which 7 were waited for; matrix products, arithmetic and copies ran while one was open for 0% of the time, Pallas kernels for 0%

profile of v2, /device:TPU:266, one launch (start us, length us, event | category | flops | bytes accessed | tf_op | source)
XLA Modules:
  0.0 192.6 jit_solution(12430876697977232007)
XLA Ops:
  0.0 1.0 copy-done.9
  1.0 0.8 copy-done.11
  1.8 0.1 shard_map.91
  1.9 4.4 %collective-permute-start = (bf16[4,8,3072]{2,1,0:T(8,128)(2,1)S(1)}, bf16[4,8,3072]{2,1,0:T(8,128)(2,1)S(1)}, u32[]{:S(2)}, u32[]{:S(2)}) collective-permute-start(bf16[4,8,3072]{2,1,0:T(8,128)(2,1)S(1)} %shard_map.91), channel_id=1, source_target_pairs={{0,0},{1,2},{2,4},{3,6},{4,8},{5,10},{6,12},{7,14},{8,16},{9,18},{... | collective-permute-start | bytes 589832 | tf_op jit(solution)/shard_map/ppermute | solution.py:152
  6.3 5.2 %collective-permute-done.local_ref = bf16[4,8,3072]{2,1,0:T(8,128)(2,1)S(1)} collective-permute-done((bf16[4,8,3072]{2,1,0:T(8,128)(2,1)S(1)}, bf16[4,8,3072]{2,1,0:T(8,128)(2,1)S(1)}, u32[]{:S(2)}, u32[]{:S(2)}) %collective-permute-start) | collective-permute-done | bytes 196640 | tf_op jit(solution)/shard_map/ppermute | solution.py:152
  11.5 0.7 copy-done.4
  12.3 0.7 copy-done.6
  13.0 0.4 shard_map.92
  13.4 0.9 copy-done.3
  14.3 2.2 %collective-permute-start.1 = (bf16[1,6144,128]{2,1,0:T(8,128)(2,1)}, bf16[1,6144,128]{2,1,0:T(8,128)(2,1)S(1)}, u32[]{:S(2)}, u32[]{:S(2)}) collective-permute-start(bf16[1,6144,128]{2,1,0:T(8,128)(2,1)} %up_near.7), channel_id=1, source_target_pairs={{0,1},{1,0},{2,3},{3,2},{4,5},{5,4},{6,7},{7,6},{8,9},{9,8},{10,11... | collective-permute-start | bytes 4718600 | tf_op jit(solution)/shard_map/ppermute | solution.py:141
  16.5 2.2 %collective-permute-start.3 = (bf16[1,128,6144]{2,1,0:T(8,128)(2,1)}, bf16[1,128,6144]{2,1,0:T(8,128)(2,1)}, u32[]{:S(2)}, u32[]{:S(2)}) collective-permute-start(bf16[1,128,6144]{2,1,0:T(8,128)(2,1)} %down_near.7), channel_id=1, source_target_pairs={{0,1},{1,0},{2,3},{3,2},{4,5},{5,4},{6,7},{7,6},{8,9},{9,8},{10,11... | collective-permute-start | bytes 4718600 | tf_op jit(solution)/shard_map/ppermute | solution.py:141
  18.6 8.9 %all-to-all-start = ((bf16[16,8,3072]{2,1,0:T(8,128)(2,1)}), bf16[16,8,3072]{2,1,0:T(8,128)(2,1)}, u32[]{:S(2)}, u32[]{:S(2)}) async-start(bf16[16,8,3072]{2,1,0:T(8,128)(2,1)} %copy-done.3), calls=%async_computation | async-start | bytes 1572864 | tf_op jit(solution)/shard_map/all_to_all | solution.py:144
  27.6 1.9 collective-permute-start.2
  29.5 1.1 collective-permute-done.2.bias_far
  30.6 8.3 %all-to-all-done = bf16[16,8,3072]{2,1,0:T(8,128)(2,1)} async-done(((bf16[16,8,3072]{2,1,0:T(8,128)(2,1)}), bf16[16,8,3072]{2,1,0:T(8,128)(2,1)}, u32[]{:S(2)}, u32[]{:S(2)}) %all-to-all-start) | async-done | bytes 786464 | tf_op jit(solution)/shard_map/all_to_all | solution.py:144
  38.9 0.0 collective-permute-done.3.down_far
  39.0 0.0 copy-start.1
  39.0 1.4 copy-done.1
  40.4 2.8 %shard_map.93 = bf16[128,3072]{1,0:T(8,128)(2,1)S(1)} custom-call(bf16[128,3072]{1,0:T(8,128)(2,1)} %bitcast.rows_ref, bf16[1,6144,128]{2,1,0:T(8,128)(2,1)S(1)} %copy-done, bf16[1,6144,128]{2,1,0:T(8,128)(2,1)S(1)} %collective-permute-done.1.up_far, bf16[1,128]{1,0:T(2,128)(2,1)S(1)} %copy-done.12, bf16[1,128]{1,0:T(2,128)(2,1)S(1)} %collective-permute-done.2.bias_far, ...), custom_call_target="tpu_custom_call" | custom-call | tf_op jit(solution)/shard_map/pallas_call | solution.py:120
  43.2 0.0 copy-start.8
  43.2 0.0 copy-start.5
  43.2 0.0 copy-start.7
  43.2 17.1 %all_to_all.40.parts_ref = bf16[16,8,3072]{2,1,0:T(8,128)(2,1)S(1)} all-to-all(bf16[16,8,3072]{2,1,0:T(8,128)(2,1)S(1)} %bitcast.10), channel_id=1, replica_groups={{0,2,4,6,8,10,12,14,16,18,20,22,24,26,28,30},{1,3,5,7,9,11,13,15,17,19,..., dimensions={0} | all-to-all | bytes 1572864 | tf_op jit(solution)/shard_map/all_to_all | solution.py:144
  60.3 0.1 shard_map.94.refs_0_
  60.5 3.1 %collective-permute-start.4 = (bf16[8,3072]{1,0:T(8,128)(2,1)S(1)}, bf16[8,3072]{1,0:T(8,128)(2,1)S(1)}, u32[]{:S(2)}, u32[]{:S(2)}) collective-permute-start(bf16[8,3072]{1,0:T(8,128)(2,1)S(1)} %shard_map.94.refs_0_), channel_id=1, source_target_pairs={{0,32},{32,64},{64,96},{96,128},{128,160},{160,192},{192,224},{224... | collective-permute-start | bytes 147464 | tf_op jit(solution)/shard_map/ppermute | solution.py:177
  63.5 4.3 %collective-permute-done.4.moved_ref = bf16[8,3072]{1,0:T(8,128)(2,1)S(1)} collective-permute-done((bf16[8,3072]{1,0:T(8,128)(2,1)S(1)}, bf16[8,3072]{1,0:T(8,128)(2,1)S(1)}, u32[]{:S(2)}, u32[]{:S(2)}) %collective-permute-start.4) | collective-permute-done | bytes 49184 | tf_op jit(solution)/shard_map/ppermute | solution.py:177
  67.8 0.4 shard_map.95
  68.2 14.8 %all_to_all.41 = bf16[16,8,3072]{2,1,0:T(8,128)(2,1)S(1)} all-to-all(bf16[16,8,3072]{2,1,0:T(8,128)(2,1)S(1)} %get-tuple-element.23), channel_id=1, replica_groups={{0,2,4,6,8,10,12,14,16,18,20,22,24,26,28,30},{1,3,5,7,9,11,13,15,17,19,..., dimensions={0} | all-to-all | bytes 1572864 | tf_op jit(solution)/shard_map/all_to_all | solution.py:144
  83.0 2.6 %shard_map.96 = bf16[128,3072]{1,0:T(8,128)(2,1)S(1)} custom-call(bf16[128,3072]{1,0:T(8,128)(2,1)S(1)} %bitcast.11, bf16[1,6144,128]{2,1,0:T(8,128)(2,1)S(1)} %copy-done, bf16[1,6144,128]{2,1,0:T(8,128)(2,1)S(1)} %collective-permute-done.1.up_far, bf16[1,128]{1,0:T(2,128)(2,1)S(1)} %copy-done.12, bf16[1,128]{1,0:T(2,128)(2,1)S(1)} %collective-permute-done.2.bias_far, ...), custom_call_target="tpu_custom_call" | custom-call | tf_op jit(solution)/shard_map/pallas_call | solution.py:120
  85.5 14.7 %all_to_all.42.parts_ref = bf16[16,8,3072]{2,1,0:T(8,128)(2,1)S(1)} all-to-all(bf16[16,8,3072]{2,1,0:T(8,128)(2,1)S(1)} %bitcast.12), channel_id=1, replica_groups={{0,2,4,6,8,10,12,14,16,18,20,22,24,26,28,30},{1,3,5,7,9,11,13,15,17,19,..., dimensions={0} | all-to-all | bytes 1572864 | tf_op jit(solution)/shard_map/all_to_all | solution.py:144
  100.3 0.1 shard_map.97.refs_1_
  100.4 1.9 collective-permute-start.5
  102.4 5.3 %collective-permute-done.5.moved_ref = bf16[8,3072]{1,0:T(8,128)(2,1)S(1)} collective-permute-done((bf16[8,3072]{1,0:T(8,128)(2,1)S(1)}, bf16[8,3072]{1,0:T(8,128)(2,1)S(1)}, u32[]{:S(2)}, u32[]{:S(2)}) %collective-permute-start.5) | collective-permute-done | bytes 49184 | tf_op jit(solution)/shard_map/ppermute | solution.py:177
  107.6 0.4 shard_map.98
  108.1 14.8 %all_to_all.43 = bf16[16,8,3072]{2,1,0:T(8,128)(2,1)S(1)} all-to-all(bf16[16,8,3072]{2,1,0:T(8,128)(2,1)S(1)} %get-tuple-element.25), channel_id=1, replica_groups={{0,2,4,6,8,10,12,14,16,18,20,22,24,26,28,30},{1,3,5,7,9,11,13,15,17,19,..., dimensions={0} | all-to-all | bytes 1572864 | tf_op jit(solution)/shard_map/all_to_all | solution.py:144
  122.8 2.6 %shard_map.99 = bf16[128,3072]{1,0:T(8,128)(2,1)S(1)} custom-call(bf16[128,3072]{1,0:T(8,128)(2,1)S(1)} %bitcast.13, bf16[1,6144,128]{2,1,0:T(8,128)(2,1)S(1)} %copy-done, bf16[1,6144,128]{2,1,0:T(8,128)(2,1)S(1)} %collective-permute-done.1.up_far, bf16[1,128]{1,0:T(2,128)(2,1)S(1)} %copy-done.12, bf16[1,128]{1,0:T(2,128)(2,1)S(1)} %collective-permute-done.2.bias_far, ...), custom_call_target="tpu_custom_call" | custom-call | tf_op jit(solution)/shard_map/pallas_call | solution.py:120
  125.4 14.8 %all_to_all.44.parts_ref = bf16[16,8,3072]{2,1,0:T(8,128)(2,1)S(1)} all-to-all(bf16[16,8,3072]{2,1,0:T(8,128)(2,1)S(1)} %bitcast.14), channel_id=1, replica_groups={{0,2,4,6,8,10,12,14,16,18,20,22,24,26,28,30},{1,3,5,7,9,11,13,15,17,19,..., dimensions={0} | all-to-all | bytes 1572864 | tf_op jit(solution)/shard_map/all_to_all | solution.py:144
  140.1 0.1 shard_map.100.refs_2_
  140.3 1.9 collective-permute-start.6
  142.2 5.3 %collective-permute-done.6.moved_ref = bf16[8,3072]{1,0:T(8,128)(2,1)S(1)} collective-permute-done((bf16[8,3072]{1,0:T(8,128)(2,1)S(1)}, bf16[8,3072]{1,0:T(8,128)(2,1)S(1)}, u32[]{:S(2)}, u32[]{:S(2)}) %collective-permute-start.6) | collective-permute-done | bytes 49184 | tf_op jit(solution)/shard_map/ppermute | solution.py:177
  147.5 0.4 shard_map.101
  147.9 14.9 %all_to_all.45 = bf16[16,8,3072]{2,1,0:T(8,128)(2,1)S(1)} all-to-all(bf16[16,8,3072]{2,1,0:T(8,128)(2,1)S(1)} %get-tuple-element.27), channel_id=1, replica_groups={{0,2,4,6,8,10,12,14,16,18,20,22,24,26,28,30},{1,3,5,7,9,11,13,15,17,19,..., dimensions={0} | all-to-all | bytes 1572864 | tf_op jit(solution)/shard_map/all_to_all | solution.py:144
  162.8 2.6 %shard_map.102 = bf16[128,3072]{1,0:T(8,128)(2,1)S(1)} custom-call(bf16[128,3072]{1,0:T(8,128)(2,1)S(1)} %bitcast.8, bf16[1,6144,128]{2,1,0:T(8,128)(2,1)S(1)} %copy-done, bf16[1,6144,128]{2,1,0:T(8,128)(2,1)S(1)} %collective-permute-done.1.up_far, bf16[1,128]{1,0:T(2,128)(2,1)S(1)} %copy-done.12, bf16[1,128]{1,0:T(2,128)(2,1)S(1)} %collective-permute-done.2.bias_far, ...), custom_call_target="tpu_custom_call" | custom-call | tf_op jit(solution)/shard_map/pallas_call | solution.py:120
  165.4 15.8 %all_to_all.46.parts_ref = bf16[16,8,3072]{2,1,0:T(8,128)(2,1)S(1)} all-to-all(bf16[16,8,3072]{2,1,0:T(8,128)(2,1)S(1)} %bitcast.9), channel_id=1, replica_groups={{0,2,4,6,8,10,12,14,16,18,20,22,24,26,28,30},{1,3,5,7,9,11,13,15,17,19,..., dimensions={0} | all-to-all | bytes 1572864 | tf_op jit(solution)/shard_map/all_to_all | solution.py:144
  181.2 0.1 shard_map.103
  181.3 1.9 collective-permute-start.7
  183.3 8.6 %collective-permute-done.7.rows_ref = bf16[4,8,3072]{2,1,0:T(8,128)(2,1)S(1)} collective-permute-done((bf16[4,8,3072]{2,1,0:T(8,128)(2,1)S(1)}, bf16[4,8,3072]{2,1,0:T(8,128)(2,1)S(1)}, u32[]{:S(2)}, u32[]{:S(2)}) %collective-permute-start.7) | collective-permute-done | bytes 196640 | tf_op jit(solution)/shard_map/ppermute | solution.py:180
  191.9 0.7 shard_map.104
  (17 shorter events, 0.0 us)
Async XLA Ops:
  0.0 38.9 %copy-start = (bf16[1,6144,128]{2,1,0:T(8,128)(2,1)S(1)}, bf16[1,6144,128]{2,1,0:T(8,128)(2,1)}, u32[]{:S(2)}) copy-start(bf16[1,6144,128]{2,1,0:T(8,128)(2,1)} %up_near.7) | copy-start | bytes 4718596
  0.0 1.0 copy-start.9
  1.0 0.8 copy-start.11
  1.9 9.6 %collective-permute-start = (bf16[4,8,3072]{2,1,0:T(8,128)(2,1)S(1)}, bf16[4,8,3072]{2,1,0:T(8,128)(2,1)S(1)}, u32[]{:S(2)}, u32[]{:S(2)}) collective-permute-start(bf16[4,8,3072]{2,1,0:T(8,128)(2,1)S(1)} %shard_map.91), channel_id=1, source_target_pairs={{0,0},{1,2},{2,4},{3,6},{4,8},{5,10},{6,12},{7,14},{8,16},{9,18},{... | collective-permute-start | bytes 589832 | tf_op jit(solution)/shard_map/ppermute | solution.py:152
  11.5 0.7 copy-start.4
  12.3 0.7 copy-start.6
  13.0 14.6 %copy-start.12 = (bf16[1,128]{1,0:T(2,128)(2,1)S(1)}, bf16[1,128]{1,0:T(2,128)(2,1)}, u32[]{:S(2)}) copy-start(bf16[1,128]{1,0:T(2,128)(2,1)} %bias_near.7) | copy-start | bytes 772
  13.0 25.9 %copy-start.10 = (s32[4,1,2,16]{3,2,1,0:T(2,128)S(1)}, s32[4,1,2,16]{3,2,1,0:T(2,128)}, u32[]{:S(2)}) copy-start(s32[4,1,2,16]{3,2,1,0:T(2,128)} %active_ref.7) | copy-start | bytes 1540
  13.4 0.9 copy-start.3
  14.3 24.6 %collective-permute-start.1 = (bf16[1,6144,128]{2,1,0:T(8,128)(2,1)}, bf16[1,6144,128]{2,1,0:T(8,128)(2,1)S(1)}, u32[]{:S(2)}, u32[]{:S(2)}) collective-permute-start(bf16[1,6144,128]{2,1,0:T(8,128)(2,1)} %up_near.7), channel_id=1, source_target_pairs={{0,1},{1,0},{2,3},{3,2},{4,5},{5,4},{6,7},{7,6},{8,9},{9,8},{10,11... | collective-permute-start | bytes 4718600 | tf_op jit(solution)/shard_map/ppermute | solution.py:141
  16.5 22.4 %collective-permute-start.3 = (bf16[1,128,6144]{2,1,0:T(8,128)(2,1)}, bf16[1,128,6144]{2,1,0:T(8,128)(2,1)}, u32[]{:S(2)}, u32[]{:S(2)}) collective-permute-start(bf16[1,128,6144]{2,1,0:T(8,128)(2,1)} %down_near.7), channel_id=1, source_target_pairs={{0,1},{1,0},{2,3},{3,2},{4,5},{5,4},{6,7},{7,6},{8,9},{9,8},{10,11... | collective-permute-start | bytes 4718600 | tf_op jit(solution)/shard_map/ppermute | solution.py:141
  18.6 20.3 %all-to-all-start = ((bf16[16,8,3072]{2,1,0:T(8,128)(2,1)}), bf16[16,8,3072]{2,1,0:T(8,128)(2,1)}, u32[]{:S(2)}, u32[]{:S(2)}) async-start(bf16[16,8,3072]{2,1,0:T(8,128)(2,1)} %copy-done.3), calls=%async_computation | async-start | bytes 1572864 | tf_op jit(solution)/shard_map/all_to_all | solution.py:144
  27.6 3.0 %collective-permute-start.2 = (bf16[1,128]{1,0:T(2,128)(2,1)S(1)}, bf16[1,128]{1,0:T(2,128)(2,1)S(1)}, u32[]{:S(2)}, u32[]{:S(2)}) collective-permute-start(bf16[1,128]{1,0:T(2,128)(2,1)S(1)} %copy-done.12), channel_id=1, source_target_pairs={{0,1},{1,0},{2,3},{3,2},{4,5},{5,4},{6,7},{7,6},{8,9},{9,8},{10,11... | collective-permute-start | bytes 776 | tf_op jit(solution)/shard_map/ppermute | solution.py:141
  39.0 1.4 copy-start.1
  43.2 17.1 %copy-start.8 = (bf16[1,6144]{1,0:T(2,128)(2,1)S(1)}, bf16[1,6144]{1,0:T(2,128)(2,1)}, u32[]{:S(2)}) copy-start(bf16[1,6144]{1,0:T(2,128)(2,1)} %bias_ref.15) | copy-start | bytes 36868
  43.2 24.6 %copy-start.5 = (bf16[1,6144]{1,0:T(2,128)(2,1)S(1)}, bf16[1,6144]{1,0:T(2,128)(2,1)}, u32[]{:S(2)}) copy-start(bf16[1,6144]{1,0:T(2,128)(2,1)} %gain_ref.7) | copy-start | bytes 36868
  43.2 24.6 %copy-start.7 = (bf16[1,6144]{1,0:T(2,128)(2,1)S(1)}, bf16[1,6144]{1,0:T(2,128)(2,1)}, u32[]{:S(2)}) copy-start(bf16[1,6144]{1,0:T(2,128)(2,1)} %bias_ref.14) | copy-start | bytes 36868
  60.3 22.7 %copy-start.2 = (bf16[1,128,6144]{2,1,0:T(8,128)(2,1)S(1)}, bf16[1,128,6144]{2,1,0:T(8,128)(2,1)}, u32[]{:S(2)}) copy-start(bf16[1,128,6144]{2,1,0:T(8,128)(2,1)} %down_near.7) | copy-start | bytes 4718596
  60.5 7.3 %collective-permute-start.4 = (bf16[8,3072]{1,0:T(8,128)(2,1)S(1)}, bf16[8,3072]{1,0:T(8,128)(2,1)S(1)}, u32[]{:S(2)}, u32[]{:S(2)}) collective-permute-start(bf16[8,3072]{1,0:T(8,128)(2,1)S(1)} %shard_map.94.refs_0_), channel_id=1, source_target_pairs={{0,32},{32,64},{64,96},{96,128},{128,160},{160,192},{192,224},{224... | collective-permute-start | bytes 147464 | tf_op jit(solution)/shard_map/ppermute | solution.py:177
  100.4 7.2 %collective-permute-start.5 = (bf16[8,3072]{1,0:T(8,128)(2,1)S(1)}, bf16[8,3072]{1,0:T(8,128)(2,1)S(1)}, u32[]{:S(2)}, u32[]{:S(2)}) collective-permute-start(bf16[8,3072]{1,0:T(8,128)(2,1)S(1)} %shard_map.97.refs_1_), channel_id=1, source_target_pairs={{0,32},{32,64},{64,96},{96,128},{128,160},{160,192},{192,224},{224... | collective-permute-start | bytes 147464 | tf_op jit(solution)/shard_map/ppermute | solution.py:177
  140.3 7.2 %collective-permute-start.6 = (bf16[8,3072]{1,0:T(8,128)(2,1)S(1)}, bf16[8,3072]{1,0:T(8,128)(2,1)S(1)}, u32[]{:S(2)}, u32[]{:S(2)}) collective-permute-start(bf16[8,3072]{1,0:T(8,128)(2,1)S(1)} %shard_map.100.refs_2_), channel_id=1, source_target_pairs={{0,32},{32,64},{64,96},{96,128},{128,160},{160,192},{192,224},{224... | collective-permute-start | bytes 147464 | tf_op jit(solution)/shard_map/ppermute | solution.py:177
  181.3 10.6 %collective-permute-start.7 = (bf16[4,8,3072]{2,1,0:T(8,128)(2,1)S(1)}, bf16[4,8,3072]{2,1,0:T(8,128)(2,1)S(1)}, u32[]{:S(2)}, u32[]{:S(2)}) collective-permute-start(bf16[4,8,3072]{2,1,0:T(8,128)(2,1)S(1)} %shard_map.103), channel_id=1, source_target_pairs={{0,0},{2,1},{4,2},{6,3},{8,4},{10,5},{12,6},{14,7},{16,8},{18,9},{... | collective-permute-start | bytes 589832 | tf_op jit(solution)/shard_map/ppermute | solution.py:180

commit v3 on v2

--- a/solution.py
+++ b/solution.py
@@ -14,6 +14,7 @@
 
 VMEM = pl.BlockSpec(memory_space=pltpu.VMEM)
 SMEM = pl.BlockSpec(memory_space=pltpu.SMEM)
+COST = pl.CostEstimate(flops=100_000, bytes_accessed=300_000, transcendentals=0)
 PARAMS = pltpu.CompilerParams(vmem_limit_bytes=40 * 1024 * 1024)
 
 
@@ -31,13 +32,24 @@
     return (part + pltpu.roll(part, 4, 0))[:, :1]
 
 
+def lay_out(rows_ref, scratch, half):
+    rows = rows_ref.astype(F32)
+    scratch[0:4] = rows[:, :half]
+    scratch[4:8] = rows[:, half:]
+    return scratch[...].astype(BF16)
+
+
 def arrange_kernel(stream_ref, arrivals_ref, out_ref, scratch):
-    half = out_ref.shape[2]
-    for item in range(TICKS):
-        rows = (stream_ref[0] if item == 0 else arrivals_ref[item - 1]).astype(F32)
-        scratch[item, 0:4] = rows[:, :half]
-        scratch[item, 4:8] = rows[:, half:]
-        out_ref[item] = scratch[item].astype(BF16)
+    for item in range(out_ref.shape[0]):
+        rows = stream_ref[0] if item == 0 else arrivals_ref[item - 1]
+        out_ref[item] = lay_out(rows, scratch, out_ref.shape[2])
+
+
+def halves_kernel(gain, bias, down_bias, gain_out, bias_out, down_bias_out):
+    half = gain_out.shape[1]
+    gain_out[...] = halves(gain, half)
+    bias_out[...] = halves(bias, half)
+    down_bias_out[...] = halves(down_bias, half)
 
 
 def norm_kernel(step, moved_ref, local_ref, gain_ref, bias_ref, rows_out, send_out):
@@ -50,7 +62,7 @@
     centred = rows - row_sum(rows) * (0.5 / half)
     var = row_sum(centred * centred) * (0.5 / half)
     scaled = centred * lax.rsqrt(var + EPS)
-    normed = (scaled * halves(gain_ref, half) + halves(bias_ref, half)).astype(BF16)
+    normed = (scaled * gain_ref[...] + bias_ref[...]).astype(BF16)
     for chip in range(CHIPS):
         send_out[chip] = normed
 
@@ -93,18 +105,22 @@
         out_ref[:, at : at + chunk] = jnp.where(low, one, two).astype(BF16)
 
 
-def sum_kernel(parts_ref, rows_ref, bias_ref, *refs):
-    before, out_ref = refs[:-1], refs[-1]
-    half = rows_ref.shape[1]
-    total = rows_ref[...].astype(F32) + halves(bias_ref, half)
+def add_up(parts_ref, rows_ref, bias_ref):
+    total = rows_ref[...].astype(F32) + bias_ref[...]
     for chip in range(CHIPS):
         total += parts_ref[chip].astype(F32)
-    if before:
-        for step, ref in enumerate(before):
-            out_ref[step] = ref[...]
-        out_ref[len(before)] = total.astype(BF16)
-    else:
-        out_ref[...] = total.astype(BF16)
+    return total.astype(BF16)
+
+
+def sum_kernel(parts_ref, rows_ref, bias_ref, out_ref):
+    out_ref[...] = add_up(parts_ref, rows_ref, bias_ref)
+
+
+def last_sum_kernel(parts_ref, rows_ref, bias_ref, *refs):
+    before, out_ref = refs[:-1], refs[-1]
+    for step, ref in enumerate(before):
+        out_ref[step] = ref[...]
+    out_ref[len(before)] = add_up(parts_ref, rows_ref, bias_ref)
 
 
 def final_kernel(rows_ref, out_ref):
@@ -115,7 +131,13 @@
         out_ref[0, step, :, half:] = rows[4:8].astype(BF16)
 
 
-def call(kernel, outs, *args, specs=None, scratch=()):
+def home_of(j):
+    x, y, core = j // 8, j // 2 % 4, j % 2
+    tile = x // 2
+    return j if core == tile else 8 * (3 - x) + 2 * y + tile
+
+
+def call(kernel, outs, *args, specs=None, scratch=(), cost=None):
     single = isinstance(outs, jax.ShapeDtypeStruct)
     return pl.pallas_call(
         kernel,
@@ -124,6 +146,7 @@
         out_specs=VMEM if single else [VMEM] * len(outs),
         scratch_shapes=list(scratch),
         compiler_params=PARAMS,
+        cost_estimate=cost,
     )(*args)
 
 
@@ -135,7 +158,8 @@
     half = width // 2
     rows_half = 2 * rows_dev
     same_core = [[2 * chip + core for chip in range(CHIPS)] for core in range(2)]
-    homes = [(j, 2 * (j % CHIPS) + j // CHIPS) for j in range(blocks)]
+    homes = [home_of(j) for j in range(blocks)]
+    go_home = list(enumerate(homes))
 
     def swap(x):
         return lax.ppermute(x, "blk", [(i, i ^ 1) for i in range(blocks)])
@@ -143,26 +167,27 @@
     def trade(x):
         return lax.all_to_all(x, "blk", 0, 0, axis_index_groups=same_core, tiled=True)
 
+    up_far, down_far = swap(up_weight), swap(down_weight)
     arranged = call(
         arrange_kernel,
         shape((TICKS, rows_half, half), BF16),
         stream, arrivals,
-        scratch=[pltpu.VMEM((TICKS, rows_half, half), F32)],
+        scratch=[pltpu.VMEM((rows_half, half), F32)],
     )
-    local = lax.ppermute(arranged, "blk", homes)
+    local = lax.ppermute(arranged, "blk", go_home)
+    gain, bias, bias_down = call(halves_kernel, [shape((rows_half, half), F32)] * 3, ln_gain, ln_bias, down_bias, cost=COST)
+    bias_far = swap(up_bias)
+    local, bias_far = lax.optimization_barrier((local, bias_far))
     moved = None
     produced = []
     for step in range(TICKS):
-        args = [local, ln_gain, ln_bias] if step == 0 else [moved, local, ln_gain, ln_bias]
+        args = [local, gain, bias]
         kernel = functools.partial(norm_kernel, step) if step else functools.partial(norm_kernel, 0, None)
         rows, outgoing = call(
             kernel,
             [shape((rows_half, half), BF16), shape((CHIPS, rows_half, half), BF16)],
-            *args,
+            *([moved] if step else []), *args,
         )
-        if step == 0:
-            outgoing, *weights = lax.optimization_barrier((outgoing, up_weight, down_weight, up_bias))
-            up_far, down_far, bias_far = map(swap, weights)
         gathered = trade(outgoing).reshape(CHIPS * rows_half, half)
         partial = call(
             functools.partial(ffn_kernel, step),
@@ -172,12 +197,12 @@
         )
         received = trade(partial.reshape(CHIPS, rows_half, half))
         if step + 1 < TICKS:
-            done = call(sum_kernel, shape((rows_half, half), BF16), received, rows, down_bias)
+            done = call(sum_kernel, shape((rows_half, half), BF16), received, rows, bias_down)
             produced.append(done)
             moved = lax.ppermute(done, "pipe", [(i, i + 1) for i in range(pipes - 1)])
         else:
-            done = call(sum_kernel, shape((TICKS, rows_half, half), BF16), received, rows, down_bias, *produced)
-    back = lax.ppermute(done, "blk", [(home, j) for j, home in homes])
+            done = call(last_sum_kernel, shape((TICKS, rows_half, half), BF16), received, rows, bias_down, *produced)
+    back = lax.ppermute(done, "blk", [(home, j) for j, home in enumerate(homes)])
     return call(final_kernel, shape((1, TICKS, rows_dev, width), BF16), back)
 
 

time: 194 us -> 181 us (0.933)
  the two profiles are of different devices: /device:TPU:266 before, /device:TPU:385 now
where the time goes in v3:
time: 181 us; the launch traced here: 180 us
  blocking collectives  113 us (62%)
  starting transfers between devices  36 us (20%)
  waiting for transfers between devices  15.6 us (9%)
  Pallas kernels  10.1 us (6%)
  local copies, waits for them, and re-layouts  5.33 us (3%)
    all_to_all x8, blocking collectives, trade(): lax.all_to_all(x, 'blk', 0, 0, axis_index_groups=same_core, tiled=True)  113 us
    ppermute x1, starting transfers between devices, on_device(): lax.ppermute(done, 'blk', [(home, j) for j, home in enumerate(homes)])  18 us
    ppermute x3, waiting for transfers between devices, on_device(): moved = lax.ppermute(done, 'pipe', [(i, i + 1) for i in range(pipes - 1)])  12.2 us
    pallas_call x15, Pallas kernels, call(): pl.pallas_call(kernel, out_shape=outs, in_specs=list(specs) if specs else...  10.1 us
    ppermute x3, starting transfers between devices, on_device(): moved = lax.ppermute(done, 'pipe', [(i, i + 1) for i in range(pipes - 1)])  6.61 us
    ppermute x3, starting transfers between devices, swap(): return lax.ppermute(x, 'blk', [(i, i ^ 1) for i in range(blocks)])  6.55 us
    unnamed x20, local copies, waits for them, and re-layouts  5.33 us
    ppermute x1, starting transfers between devices, on_device(): local = lax.ppermute(arranged, 'blk', go_home)  4.77 us
  transfers between devices with their start and end apart: 8, of which 4 were waited for; matrix products, arithmetic and copies ran while one was open for 0% of the time, Pallas kernels for 0%

profile of v3, /device:TPU:385, one launch (start us, length us, event | category | flops | bytes accessed | tf_op | source)
XLA Modules:
  0.0 180.3 jit_solution(16242479989185192404)
XLA Ops:
  0.0 2.7 %collective-permute-start.2 = (bf16[1,6144,128]{2,1,0:T(8,128)(2,1)}, bf16[1,6144,128]{2,1,0:T(8,128)(2,1)S(1)}, u32[]{:S(2)}, u32[]{:S(2)}) collective-permute-start(bf16[1,6144,128]{2,1,0:T(8,128)(2,1)} %up_near.7), channel_id=1, source_target_pairs={{0,1},{1,0},{2,3},{3,2},{4,5},{5,4},{6,7},{7,6},{8,9},{9,8},{10,11... | collective-permute-start | bytes 4718600 | tf_op jit(solution)/shard_map/ppermute | solution.py:165
  2.7 1.9 %collective-permute-start.3 = (bf16[1,128,6144]{2,1,0:T(8,128)(2,1)}, bf16[1,128,6144]{2,1,0:T(8,128)(2,1)S(1)}, u32[]{:S(2)}, u32[]{:S(2)}) collective-permute-start(bf16[1,128,6144]{2,1,0:T(8,128)(2,1)} %down_near.7), channel_id=1, source_target_pairs={{0,1},{1,0},{2,3},{3,2},{4,5},{5,4},{6,7},{7,6},{8,9},{9,8},{10,11... | collective-permute-start | bytes 4718600 | tf_op jit(solution)/shard_map/ppermute | solution.py:165
  4.7 0.9 copy-done.3
  5.6 0.8 copy-done.5
  6.4 0.1 shard_map.91
  6.4 4.8 %collective-permute-start = (bf16[4,8,3072]{2,1,0:T(8,128)(2,1)S(1)}, bf16[4,8,3072]{2,1,0:T(8,128)(2,1)S(1)}, u32[]{:S(2)}, u32[]{:S(2)}) collective-permute-start(bf16[4,8,3072]{2,1,0:T(8,128)(2,1)S(1)} %shard_map.91), channel_id=1, source_target_pairs={{0,0},{1,24},{2,2},{3,26},{4,4},{5,28},{6,6},{7,30},{8,8},{9,16},{... | collective-permute-start | bytes 589832 | tf_op jit(solution)/shard_map/ppermute | solution.py:177
  11.2 1.9 %collective-permute-start.1 = (bf16[1,128]{1,0:T(2,128)(2,1)}, bf16[1,128]{1,0:T(2,128)(2,1)S(1)}, u32[]{:S(2)}, u32[]{:S(2)}) collective-permute-start(bf16[1,128]{1,0:T(2,128)(2,1)} %bias_near.7), channel_id=1, source_target_pairs={{0,1},{1,0},{2,3},{3,2},{4,5},{5,4},{6,7},{7,6},{8,9},{9,8},{10,11... | collective-permute-start | bytes 776 | tf_op jit(solution)/shard_map/ppermute | solution.py:165
  13.2 0.0 copy-start.6
  13.2 0.7 copy-done.6
  13.9 0.7 copy-done.7
  14.6 0.7 copy-done.8
  15.4 0.1 shard_map.92
  15.4 0.0 collective-permute-done.1.bias_far
  15.5 0.0 collective-permute-done.local_ref
  15.5 0.4 shard_map.93
  15.9 16.1 %all_to_all.40 = bf16[16,8,3072]{2,1,0:T(8,128)(2,1)S(1)} all-to-all(bf16[16,8,3072]{2,1,0:T(8,128)(2,1)S(1)} %get-tuple-element.21), channel_id=1, replica_groups={{0,2,4,6,8,10,12,14,16,18,20,22,24,26,28,30},{1,3,5,7,9,11,13,15,17,19,..., dimensions={0} | all-to-all | bytes 1572864 | tf_op jit(solution)/shard_map/all_to_all | solution.py:168
  32.0 0.0 collective-permute-done.2.up_far
  32.0 0.0 collective-permute-done.3.down_far
  32.0 0.0 copy-done
  32.0 0.0 copy-start.1
  32.0 1.4 copy-done.1
  33.4 1.8 shard_map.94
  35.2 14.2 %all_to_all.41.parts_ref = bf16[16,8,3072]{2,1,0:T(8,128)(2,1)S(1)} all-to-all(bf16[16,8,3072]{2,1,0:T(8,128)(2,1)S(1)} %bitcast.11), channel_id=1, replica_groups={{0,2,4,6,8,10,12,14,16,18,20,22,24,26,28,30},{1,3,5,7,9,11,13,15,17,19,..., dimensions={0} | all-to-all | bytes 1572864 | tf_op jit(solution)/shard_map/all_to_all | solution.py:168
  49.4 0.1 shard_map.95.refs_0_
  49.5 2.8 %collective-permute-start.4 = (bf16[8,3072]{1,0:T(8,128)(2,1)S(1)}, bf16[8,3072]{1,0:T(8,128)(2,1)S(1)}, u32[]{:S(2)}, u32[]{:S(2)}) collective-permute-start(bf16[8,3072]{1,0:T(8,128)(2,1)S(1)} %shard_map.95.refs_0_), channel_id=1, source_target_pairs={{0,32},{32,64},{64,96},{96,128},{128,160},{160,192},{192,224},{224... | collective-permute-start | bytes 147464 | tf_op jit(solution)/shard_map/ppermute | solution.py:202
  52.3 3.4 %collective-permute-done.4.moved_ref = bf16[8,3072]{1,0:T(8,128)(2,1)S(1)} collective-permute-done((bf16[8,3072]{1,0:T(8,128)(2,1)S(1)}, bf16[8,3072]{1,0:T(8,128)(2,1)S(1)}, u32[]{:S(2)}, u32[]{:S(2)}) %collective-permute-start.4) | collective-permute-done | bytes 49184 | tf_op jit(solution)/shard_map/ppermute | solution.py:202
  55.7 0.4 shard_map.96
  56.1 13.8 %all_to_all.42 = bf16[16,8,3072]{2,1,0:T(8,128)(2,1)S(1)} all-to-all(bf16[16,8,3072]{2,1,0:T(8,128)(2,1)S(1)} %get-tuple-element.25), channel_id=1, replica_groups={{0,2,4,6,8,10,12,14,16,18,20,22,24,26,28,30},{1,3,5,7,9,11,13,15,17,19,..., dimensions={0} | all-to-all | bytes 1572864 | tf_op jit(solution)/shard_map/all_to_all | solution.py:168
  69.9 1.8 shard_map.97
  71.7 13.3 %all_to_all.43.parts_ref = bf16[16,8,3072]{2,1,0:T(8,128)(2,1)S(1)} all-to-all(bf16[16,8,3072]{2,1,0:T(8,128)(2,1)S(1)} %bitcast.13), channel_id=1, replica_groups={{0,2,4,6,8,10,12,14,16,18,20,22,24,26,28,30},{1,3,5,7,9,11,13,15,17,19,..., dimensions={0} | all-to-all | bytes 1572864 | tf_op jit(solution)/shard_map/all_to_all | solution.py:168
  85.0 0.1 shard_map.98.refs_1_
  85.1 1.9 %collective-permute-start.5 = (bf16[8,3072]{1,0:T(8,128)(2,1)S(1)}, bf16[8,3072]{1,0:T(8,128)(2,1)S(1)}, u32[]{:S(2)}, u32[]{:S(2)}) collective-permute-start(bf16[8,3072]{1,0:T(8,128)(2,1)S(1)} %shard_map.98.refs_1_), channel_id=1, source_target_pairs={{0,32},{32,64},{64,96},{96,128},{128,160},{160,192},{192,224},{224... | collective-permute-start | bytes 147464 | tf_op jit(solution)/shard_map/ppermute | solution.py:202
  87.1 4.4 %collective-permute-done.5.moved_ref = bf16[8,3072]{1,0:T(8,128)(2,1)S(1)} collective-permute-done((bf16[8,3072]{1,0:T(8,128)(2,1)S(1)}, bf16[8,3072]{1,0:T(8,128)(2,1)S(1)}, u32[]{:S(2)}, u32[]{:S(2)}) %collective-permute-start.5) | collective-permute-done | bytes 49184 | tf_op jit(solution)/shard_map/ppermute | solution.py:202
  91.5 0.4 shard_map.99
  91.9 13.3 %all_to_all.44 = bf16[16,8,3072]{2,1,0:T(8,128)(2,1)S(1)} all-to-all(bf16[16,8,3072]{2,1,0:T(8,128)(2,1)S(1)} %get-tuple-element.27), channel_id=1, replica_groups={{0,2,4,6,8,10,12,14,16,18,20,22,24,26,28,30},{1,3,5,7,9,11,13,15,17,19,..., dimensions={0} | all-to-all | bytes 1572864 | tf_op jit(solution)/shard_map/all_to_all | solution.py:168
  105.2 1.8 shard_map.100
  107.0 13.3 %all_to_all.45.parts_ref = bf16[16,8,3072]{2,1,0:T(8,128)(2,1)S(1)} all-to-all(bf16[16,8,3072]{2,1,0:T(8,128)(2,1)S(1)} %bitcast.15), channel_id=1, replica_groups={{0,2,4,6,8,10,12,14,16,18,20,22,24,26,28,30},{1,3,5,7,9,11,13,15,17,19,..., dimensions={0} | all-to-all | bytes 1572864 | tf_op jit(solution)/shard_map/all_to_all | solution.py:168
  120.3 0.1 shard_map.101.refs_2_
  120.4 1.9 %collective-permute-start.6 = (bf16[8,3072]{1,0:T(8,128)(2,1)S(1)}, bf16[8,3072]{1,0:T(8,128)(2,1)S(1)}, u32[]{:S(2)}, u32[]{:S(2)}) collective-permute-start(bf16[8,3072]{1,0:T(8,128)(2,1)S(1)} %shard_map.101.refs_2_), channel_id=1, source_target_pairs={{0,32},{32,64},{64,96},{96,128},{128,160},{160,192},{192,224},{224... | collective-permute-start | bytes 147464 | tf_op jit(solution)/shard_map/ppermute | solution.py:202
  122.4 4.4 %collective-permute-done.6.moved_ref = bf16[8,3072]{1,0:T(8,128)(2,1)S(1)} collective-permute-done((bf16[8,3072]{1,0:T(8,128)(2,1)S(1)}, bf16[8,3072]{1,0:T(8,128)(2,1)S(1)}, u32[]{:S(2)}, u32[]{:S(2)}) %collective-permute-start.6) | collective-permute-done | bytes 49184 | tf_op jit(solution)/shard_map/ppermute | solution.py:202
  126.8 0.4 shard_map.102
  127.2 13.3 %all_to_all.46 = bf16[16,8,3072]{2,1,0:T(8,128)(2,1)S(1)} all-to-all(bf16[16,8,3072]{2,1,0:T(8,128)(2,1)S(1)} %get-tuple-element.29), channel_id=1, replica_groups={{0,2,4,6,8,10,12,14,16,18,20,22,24,26,28,30},{1,3,5,7,9,11,13,15,17,19,..., dimensions={0} | all-to-all | bytes 1572864 | tf_op jit(solution)/shard_map/all_to_all | solution.py:168
  140.5 1.8 shard_map.103
  142.3 15.8 %all_to_all.47.parts_ref = bf16[16,8,3072]{2,1,0:T(8,128)(2,1)S(1)} all-to-all(bf16[16,8,3072]{2,1,0:T(8,128)(2,1)S(1)} %bitcast.10), channel_id=1, replica_groups={{0,2,4,6,8,10,12,14,16,18,20,22,24,26,28,30},{1,3,5,7,9,11,13,15,17,19,..., dimensions={0} | all-to-all | bytes 1572864 | tf_op jit(solution)/shard_map/all_to_all | solution.py:168
  158.1 0.1 shard_map.104
  158.3 18.0 %collective-permute-start.7 = (bf16[4,8,3072]{2,1,0:T(8,128)(2,1)S(1)}, bf16[4,8,3072]{2,1,0:T(8,128)(2,1)S(1)}, u32[]{:S(2)}, u32[]{:S(2)}) collective-permute-start(bf16[4,8,3072]{2,1,0:T(8,128)(2,1)S(1)} %shard_map.104), channel_id=1, source_target_pairs={{0,0},{24,1},{2,2},{26,3},{4,4},{28,5},{6,6},{30,7},{8,8},{16,9},{... | collective-permute-start | bytes 589832 | tf_op jit(solution)/shard_map/ppermute | solution.py:205
  176.3 3.3 %collective-permute-done.7.rows_ref = bf16[4,8,3072]{2,1,0:T(8,128)(2,1)S(1)} collective-permute-done((bf16[4,8,3072]{2,1,0:T(8,128)(2,1)S(1)}, bf16[4,8,3072]{2,1,0:T(8,128)(2,1)S(1)}, u32[]{:S(2)}, u32[]{:S(2)}) %collective-permute-start.7) | collective-permute-done | bytes 196640 | tf_op jit(solution)/shard_map/ppermute | solution.py:205
  179.6 0.7 shard_map.105
  (11 shorter events, 0.0 us)
Async XLA Ops:
  0.0 32.0 %copy-start = (bf16[1,6144,128]{2,1,0:T(8,128)(2,1)S(1)}, bf16[1,6144,128]{2,1,0:T(8,128)(2,1)}, u32[]{:S(2)}) copy-start(bf16[1,6144,128]{2,1,0:T(8,128)(2,1)} %up_near.7) | copy-start | bytes 4718596
  0.0 32.0 %collective-permute-start.2 = (bf16[1,6144,128]{2,1,0:T(8,128)(2,1)}, bf16[1,6144,128]{2,1,0:T(8,128)(2,1)S(1)}, u32[]{:S(2)}, u32[]{:S(2)}) collective-permute-start(bf16[1,6144,128]{2,1,0:T(8,128)(2,1)} %up_near.7), channel_id=1, source_target_pairs={{0,1},{1,0},{2,3},{3,2},{4,5},{5,4},{6,7},{7,6},{8,9},{9,8},{10,11... | collective-permute-start | bytes 4718600 | tf_op jit(solution)/shard_map/ppermute | solution.py:165
  2.7 29.2 %collective-permute-start.3 = (bf16[1,128,6144]{2,1,0:T(8,128)(2,1)}, bf16[1,128,6144]{2,1,0:T(8,128)(2,1)S(1)}, u32[]{:S(2)}, u32[]{:S(2)}) collective-permute-start(bf16[1,128,6144]{2,1,0:T(8,128)(2,1)} %down_near.7), channel_id=1, source_target_pairs={{0,1},{1,0},{2,3},{3,2},{4,5},{5,4},{6,7},{7,6},{8,9},{9,8},{10,11... | collective-permute-start | bytes 4718600 | tf_op jit(solution)/shard_map/ppermute | solution.py:165
  4.6 0.9 copy-start.3
  5.6 0.8 copy-start.5
  6.4 25.6 %copy-start.4 = (s32[4,1,2,16]{3,2,1,0:T(2,128)S(1)}, s32[4,1,2,16]{3,2,1,0:T(2,128)}, u32[]{:S(2)}) copy-start(s32[4,1,2,16]{3,2,1,0:T(2,128)} %active_ref.7) | copy-start | bytes 1540
  6.4 9.0 %collective-permute-start = (bf16[4,8,3072]{2,1,0:T(8,128)(2,1)S(1)}, bf16[4,8,3072]{2,1,0:T(8,128)(2,1)S(1)}, u32[]{:S(2)}, u32[]{:S(2)}) collective-permute-start(bf16[4,8,3072]{2,1,0:T(8,128)(2,1)S(1)} %shard_map.91), channel_id=1, source_target_pairs={{0,0},{1,24},{2,2},{3,26},{4,4},{5,28},{6,6},{7,30},{8,8},{9,16},{... | collective-permute-start | bytes 589832 | tf_op jit(solution)/shard_map/ppermute | solution.py:177
  11.2 4.2 %collective-permute-start.1 = (bf16[1,128]{1,0:T(2,128)(2,1)}, bf16[1,128]{1,0:T(2,128)(2,1)S(1)}, u32[]{:S(2)}, u32[]{:S(2)}) collective-permute-start(bf16[1,128]{1,0:T(2,128)(2,1)} %bias_near.7), channel_id=1, source_target_pairs={{0,1},{1,0},{2,3},{3,2},{4,5},{5,4},{6,7},{7,6},{8,9},{9,8},{10,11... | collective-permute-start | bytes 776 | tf_op jit(solution)/shard_map/ppermute | solution.py:165
  13.2 0.7 copy-start.6
  13.9 0.7 copy-start.7
  14.6 0.7 copy-start.8
  15.4 16.6 %copy-start.9 = (bf16[1,128]{1,0:T(2,128)(2,1)S(1)}, bf16[1,128]{1,0:T(2,128)(2,1)}, u32[]{:S(2)}) copy-start(bf16[1,128]{1,0:T(2,128)(2,1)} %bias_near.7) | copy-start | bytes 772
  32.0 1.4 copy-start.1
  49.4 20.5 %copy-start.2 = (bf16[1,128,6144]{2,1,0:T(8,128)(2,1)S(1)}, bf16[1,128,6144]{2,1,0:T(8,128)(2,1)}, u32[]{:S(2)}) copy-start(bf16[1,128,6144]{2,1,0:T(8,128)(2,1)} %down_near.7) | copy-start | bytes 4718596
  49.5 6.2 %collective-permute-start.4 = (bf16[8,3072]{1,0:T(8,128)(2,1)S(1)}, bf16[8,3072]{1,0:T(8,128)(2,1)S(1)}, u32[]{:S(2)}, u32[]{:S(2)}) collective-permute-start(bf16[8,3072]{1,0:T(8,128)(2,1)S(1)} %shard_map.95.refs_0_), channel_id=1, source_target_pairs={{0,32},{32,64},{64,96},{96,128},{128,160},{160,192},{192,224},{224... | collective-permute-start | bytes 147464 | tf_op jit(solution)/shard_map/ppermute | solution.py:202
  85.1 6.3 %collective-permute-start.5 = (bf16[8,3072]{1,0:T(8,128)(2,1)S(1)}, bf16[8,3072]{1,0:T(8,128)(2,1)S(1)}, u32[]{:S(2)}, u32[]{:S(2)}) collective-permute-start(bf16[8,3072]{1,0:T(8,128)(2,1)S(1)} %shard_map.98.refs_1_), channel_id=1, source_target_pairs={{0,32},{32,64},{64,96},{96,128},{128,160},{160,192},{192,224},{224... | collective-permute-start | bytes 147464 | tf_op jit(solution)/shard_map/ppermute | solution.py:202
  120.4 6.3 %collective-permute-start.6 = (bf16[8,3072]{1,0:T(8,128)(2,1)S(1)}, bf16[8,3072]{1,0:T(8,128)(2,1)S(1)}, u32[]{:S(2)}, u32[]{:S(2)}) collective-permute-start(bf16[8,3072]{1,0:T(8,128)(2,1)S(1)} %shard_map.101.refs_2_), channel_id=1, source_target_pairs={{0,32},{32,64},{64,96},{96,128},{128,160},{160,192},{192,224},{224... | collective-permute-start | bytes 147464 | tf_op jit(solution)/shard_map/ppermute | solution.py:202
  158.3 21.4 %collective-permute-start.7 = (bf16[4,8,3072]{2,1,0:T(8,128)(2,1)S(1)}, bf16[4,8,3072]{2,1,0:T(8,128)(2,1)S(1)}, u32[]{:S(2)}, u32[]{:S(2)}) collective-permute-start(bf16[4,8,3072]{2,1,0:T(8,128)(2,1)S(1)} %shard_map.104), channel_id=1, source_target_pairs={{0,0},{24,1},{2,2},{26,3},{4,4},{28,5},{6,6},{30,7},{8,8},{16,9},{... | collective-permute-start | bytes 589832 | tf_op jit(solution)/shard_map/ppermute | solution.py:205

commit v4 on v3

--- a/solution.py
+++ b/solution.py
@@ -45,11 +45,10 @@
         out_ref[item] = lay_out(rows, scratch, out_ref.shape[2])
 
 
-def halves_kernel(gain, bias, down_bias, gain_out, bias_out, down_bias_out):
+def halves_kernel(gain, bias, gain_out, bias_out):
     half = gain_out.shape[1]
     gain_out[...] = halves(gain, half)
     bias_out[...] = halves(bias, half)
-    down_bias_out[...] = halves(down_bias, half)
 
 
 def norm_kernel(step, moved_ref, local_ref, gain_ref, bias_ref, rows_out, send_out):
@@ -106,7 +105,7 @@
 
 
 def add_up(parts_ref, rows_ref, bias_ref):
-    total = rows_ref[...].astype(F32) + bias_ref[...]
+    total = rows_ref[...].astype(F32) + halves(bias_ref, rows_ref.shape[1])
     for chip in range(CHIPS):
         total += parts_ref[chip].astype(F32)
     return total.astype(BF16)
@@ -157,7 +156,8 @@
     rows_dev, width = stream.shape[1], stream.shape[2]
     half = width // 2
     rows_half = 2 * rows_dev
-    same_core = [[2 * chip + core for chip in range(CHIPS)] for core in range(2)]
+    by_core = (lambda k: 8 * (k % 4) + 2 * (k // 4), lambda k: 2 * k + 1)
+    same_core = [[device(k) for k in range(CHIPS)] for device in by_core]
     homes = [home_of(j) for j in range(blocks)]
     go_home = list(enumerate(homes))
 
@@ -175,7 +175,7 @@
         scratch=[pltpu.VMEM((rows_half, half), F32)],
     )
     local = lax.ppermute(arranged, "blk", go_home)
-    gain, bias, bias_down = call(halves_kernel, [shape((rows_half, half), F32)] * 3, ln_gain, ln_bias, down_bias, cost=COST)
+    gain, bias = call(halves_kernel, [shape((rows_half, half), F32)] * 2, ln_gain, ln_bias, cost=COST)
     bias_far = swap(up_bias)
     local, bias_far = lax.optimization_barrier((local, bias_far))
     moved = None
@@ -197,11 +197,11 @@
         )
         received = trade(partial.reshape(CHIPS, rows_half, half))
         if step + 1 < TICKS:
-            done = call(sum_kernel, shape((rows_half, half), BF16), received, rows, bias_down)
+            done = call(sum_kernel, shape((rows_half, half), BF16), received, rows, down_bias)
             produced.append(done)
             moved = lax.ppermute(done, "pipe", [(i, i + 1) for i in range(pipes - 1)])
         else:
-            done = call(last_sum_kernel, shape((TICKS, rows_half, half), BF16), received, rows, bias_down, *produced)
+            done = call(last_sum_kernel, shape((TICKS, rows_half, half), BF16), received, rows, down_bias, *produced)
     back = lax.ppermute(done, "blk", [(home, j) for j, home in enumerate(homes)])
     return call(final_kernel, shape((1, TICKS, rows_dev, width), BF16), back)
 

time: 181 us -> 178 us (0.983)
  the two profiles are of different devices: /device:TPU:385 before, /device:TPU:1 now
where the time goes in v4:
time: 178 us; the launch traced here: 177 us
  blocking collectives  118 us (66%)
  starting transfers between devices  34.5 us (19%)
  Pallas kernels  10.2 us (6%)
  waiting for transfers between devices  9.62 us (5%)
  local copies, waits for them, and re-layouts  4.59 us (3%)
    all_to_all x8, blocking collectives, trade(): lax.all_to_all(x, 'blk', 0, 0, axis_index_groups=same_core, tiled=True)  118 us
    ppermute x3, starting transfers between devices, swap(): return lax.ppermute(x, 'blk', [(i, i ^ 1) for i in range(blocks)])  12.8 us
    ppermute x1, starting transfers between devices, on_device(): lax.ppermute(done, 'blk', [(home, j) for j, home in enumerate(homes)])  12.5 us
    pallas_call x15, Pallas kernels, call(): pl.pallas_call(kernel, out_shape=outs, in_specs=list(specs) if specs else...  10.2 us
    ppermute x3, starting transfers between devices, on_device(): moved = lax.ppermute(done, 'pipe', [(i, i + 1) for i in range(pipes - 1)])  7.35 us
    unnamed x20, local copies, waits for them, and re-layouts  4.59 us
  transfers between devices with their start and end apart: 8, of which 5 were waited for; matrix products, arithmetic and copies ran while one was open for 0% of the time, Pallas kernels for 0%

profile of v4, /device:TPU:1, one launch (start us, length us, event | category | flops | bytes accessed | tf_op | source)
XLA Modules:
  0.0 177.3 jit_solution(8708425936825415313)
XLA Ops:
  0.0 8.9 %collective-permute-start.2 = (bf16[1,6144,128]{2,1,0:T(8,128)(2,1)}, bf16[1,6144,128]{2,1,0:T(8,128)(2,1)S(1)}, u32[]{:S(2)}, u32[]{:S(2)}) collective-permute-start(bf16[1,6144,128]{2,1,0:T(8,128)(2,1)} %up_near.7), channel_id=1, source_target_pairs={{0,1},{1,0},{2,3},{3,2},{4,5},{5,4},{6,7},{7,6},{8,9},{9,8},{10,11... | collective-permute-start | bytes 4718600 | tf_op jit(solution)/shard_map/ppermute | solution.py:165
  8.9 1.9 %collective-permute-start.3 = (bf16[1,128,6144]{2,1,0:T(8,128)(2,1)}, bf16[1,128,6144]{2,1,0:T(8,128)(2,1)S(1)}, u32[]{:S(2)}, u32[]{:S(2)}) collective-permute-start(bf16[1,128,6144]{2,1,0:T(8,128)(2,1)} %down_near.7), channel_id=1, source_target_pairs={{0,1},{1,0},{2,3},{3,2},{4,5},{5,4},{6,7},{7,6},{8,9},{9,8},{10,11... | collective-permute-start | bytes 4718600 | tf_op jit(solution)/shard_map/ppermute | solution.py:165
  10.8 0.0 copy-start.4
  10.9 0.9 copy-done.4
  11.8 0.8 copy-done.6
  12.6 0.1 shard_map.91
  12.7 1.9 %collective-permute-start = (bf16[4,8,3072]{2,1,0:T(8,128)(2,1)S(1)}, bf16[4,8,3072]{2,1,0:T(8,128)(2,1)S(1)}, u32[]{:S(2)}, u32[]{:S(2)}) collective-permute-start(bf16[4,8,3072]{2,1,0:T(8,128)(2,1)S(1)} %shard_map.91), channel_id=1, source_target_pairs={{0,0},{1,24},{2,2},{3,26},{4,4},{5,28},{6,6},{7,30},{8,8},{9,16},{... | collective-permute-start | bytes 589832 | tf_op jit(solution)/shard_map/ppermute | solution.py:177
  14.6 1.9 %collective-permute-start.1 = (bf16[1,128]{1,0:T(2,128)(2,1)}, bf16[1,128]{1,0:T(2,128)(2,1)S(1)}, u32[]{:S(2)}, u32[]{:S(2)}) collective-permute-start(bf16[1,128]{1,0:T(2,128)(2,1)} %bias_near.7), channel_id=1, source_target_pairs={{0,1},{1,0},{2,3},{3,2},{4,5},{5,4},{6,7},{7,6},{8,9},{9,8},{10,11... | collective-permute-start | bytes 776 | tf_op jit(solution)/shard_map/ppermute | solution.py:165
  16.5 0.0 copy-start.7
  16.5 0.7 copy-done.7
  17.3 0.7 copy-done.8
  18.0 0.0 collective-permute-done.1.bias_far
  18.1 2.8 %collective-permute-done.local_ref = bf16[4,8,3072]{2,1,0:T(8,128)(2,1)S(1)} collective-permute-done((bf16[4,8,3072]{2,1,0:T(8,128)(2,1)S(1)}, bf16[4,8,3072]{2,1,0:T(8,128)(2,1)S(1)}, u32[]{:S(2)}, u32[]{:S(2)}) %collective-permute-start) | collective-permute-done | bytes 196640 | tf_op jit(solution)/shard_map/ppermute | solution.py:177
  20.9 0.4 shard_map.93
  21.3 16.6 %all_to_all.40 = bf16[16,8,3072]{2,1,0:T(8,128)(2,1)S(1)} all-to-all(bf16[16,8,3072]{2,1,0:T(8,128)(2,1)S(1)} %get-tuple-element.20), channel_id=1, replica_groups={{0,8,16,24,2,10,18,26,4,12,20,28,6,14,22,30},{1,3,5,7,9,11,13,15,17,19,..., dimensions={0} | all-to-all | bytes 1572864 | tf_op jit(solution)/shard_map/all_to_all | solution.py:168
  37.9 0.0 collective-permute-done.2.up_far
  37.9 0.0 collective-permute-done.3.down_far
  37.9 0.0 copy-start.1
  38.0 1.4 copy-done.1
  39.4 1.8 %shard_map.94 = bf16[128,3072]{1,0:T(8,128)(2,1)S(1)} custom-call(bf16[128,3072]{1,0:T(8,128)(2,1)S(1)} %bitcast.8, bf16[1,6144,128]{2,1,0:T(8,128)(2,1)S(1)} %copy-done, bf16[1,6144,128]{2,1,0:T(8,128)(2,1)S(1)} %collective-permute-done.2.up_far, bf16[1,128]{1,0:T(2,128)(2,1)S(1)} %copy-done.9, bf16[1,128]{1,0:T(2,128)(2,1)S(1)} %collective-permute-done.1.bias_far, ...), custom_call_target="tpu_custom_call" | custom-call | tf_op jit(solution)/shard_map/pallas_call | solution.py:141
  41.1 0.0 copy-start.3
  41.2 16.4 %all_to_all.41.parts_ref = bf16[16,8,3072]{2,1,0:T(8,128)(2,1)S(1)} all-to-all(bf16[16,8,3072]{2,1,0:T(8,128)(2,1)S(1)} %bitcast.11), channel_id=1, replica_groups={{0,8,16,24,2,10,18,26,4,12,20,28,6,14,22,30},{1,3,5,7,9,11,13,15,17,19,..., dimensions={0} | all-to-all | bytes 1572864 | tf_op jit(solution)/shard_map/all_to_all | solution.py:168
  57.5 0.0 copy-done.3
  57.5 0.1 shard_map.95.refs_0_
  57.7 1.4 collective-permute-start.4
  59.1 1.2 collective-permute-done.4.moved_ref
  60.3 0.4 shard_map.96
  60.7 16.0 %all_to_all.42 = bf16[16,8,3072]{2,1,0:T(8,128)(2,1)S(1)} all-to-all(bf16[16,8,3072]{2,1,0:T(8,128)(2,1)S(1)} %get-tuple-element.23), channel_id=1, replica_groups={{0,8,16,24,2,10,18,26,4,12,20,28,6,14,22,30},{1,3,5,7,9,11,13,15,17,19,..., dimensions={0} | all-to-all | bytes 1572864 | tf_op jit(solution)/shard_map/all_to_all | solution.py:168
  76.7 1.8 %shard_map.97 = bf16[128,3072]{1,0:T(8,128)(2,1)S(1)} custom-call(bf16[128,3072]{1,0:T(8,128)(2,1)S(1)} %bitcast.12, bf16[1,6144,128]{2,1,0:T(8,128)(2,1)S(1)} %copy-done, bf16[1,6144,128]{2,1,0:T(8,128)(2,1)S(1)} %collective-permute-done.2.up_far, bf16[1,128]{1,0:T(2,128)(2,1)S(1)} %copy-done.9, bf16[1,128]{1,0:T(2,128)(2,1)S(1)} %collective-permute-done.1.bias_far, ...), custom_call_target="tpu_custom_call" | custom-call | tf_op jit(solution)/shard_map/pallas_call | solution.py:141
  78.5 15.8 %all_to_all.43.parts_ref = bf16[16,8,3072]{2,1,0:T(8,128)(2,1)S(1)} all-to-all(bf16[16,8,3072]{2,1,0:T(8,128)(2,1)S(1)} %bitcast.13), channel_id=1, replica_groups={{0,8,16,24,2,10,18,26,4,12,20,28,6,14,22,30},{1,3,5,7,9,11,13,15,17,19,..., dimensions={0} | all-to-all | bytes 1572864 | tf_op jit(solution)/shard_map/all_to_all | solution.py:168
  94.3 0.1 shard_map.98.refs_1_
  94.4 2.3 %collective-permute-start.5 = (bf16[8,3072]{1,0:T(8,128)(2,1)S(1)}, bf16[8,3072]{1,0:T(8,128)(2,1)S(1)}, u32[]{:S(2)}, u32[]{:S(2)}) collective-permute-start(bf16[8,3072]{1,0:T(8,128)(2,1)S(1)} %shard_map.98.refs_1_), channel_id=1, source_target_pairs={{0,32},{32,64},{64,96},{96,128},{128,160},{160,192},{192,224},{224... | collective-permute-start | bytes 147464 | tf_op jit(solution)/shard_map/ppermute | solution.py:202
  96.7 1.2 collective-permute-done.5.moved_ref
  97.8 0.4 shard_map.99
  98.3 13.1 %all_to_all.44 = bf16[16,8,3072]{2,1,0:T(8,128)(2,1)S(1)} all-to-all(bf16[16,8,3072]{2,1,0:T(8,128)(2,1)S(1)} %get-tuple-element.25), channel_id=1, replica_groups={{0,8,16,24,2,10,18,26,4,12,20,28,6,14,22,30},{1,3,5,7,9,11,13,15,17,19,..., dimensions={0} | all-to-all | bytes 1572864 | tf_op jit(solution)/shard_map/all_to_all | solution.py:168
  111.3 1.8 %shard_map.100 = bf16[128,3072]{1,0:T(8,128)(2,1)S(1)} custom-call(bf16[128,3072]{1,0:T(8,128)(2,1)S(1)} %bitcast.14, bf16[1,6144,128]{2,1,0:T(8,128)(2,1)S(1)} %copy-done, bf16[1,6144,128]{2,1,0:T(8,128)(2,1)S(1)} %collective-permute-done.2.up_far, bf16[1,128]{1,0:T(2,128)(2,1)S(1)} %copy-done.9, bf16[1,128]{1,0:T(2,128)(2,1)S(1)} %collective-permute-done.1.bias_far, ...), custom_call_target="tpu_custom_call" | custom-call | tf_op jit(solution)/shard_map/pallas_call | solution.py:141
  113.1 13.6 %all_to_all.45.parts_ref = bf16[16,8,3072]{2,1,0:T(8,128)(2,1)S(1)} all-to-all(bf16[16,8,3072]{2,1,0:T(8,128)(2,1)S(1)} %bitcast.15), channel_id=1, replica_groups={{0,8,16,24,2,10,18,26,4,12,20,28,6,14,22,30},{1,3,5,7,9,11,13,15,17,19,..., dimensions={0} | all-to-all | bytes 1572864 | tf_op jit(solution)/shard_map/all_to_all | solution.py:168
  126.8 0.1 shard_map.101.refs_2_
  126.9 3.7 %collective-permute-start.6 = (bf16[8,3072]{1,0:T(8,128)(2,1)S(1)}, bf16[8,3072]{1,0:T(8,128)(2,1)S(1)}, u32[]{:S(2)}, u32[]{:S(2)}) collective-permute-start(bf16[8,3072]{1,0:T(8,128)(2,1)S(1)} %shard_map.101.refs_2_), channel_id=1, source_target_pairs={{0,32},{32,64},{64,96},{96,128},{128,160},{160,192},{192,224},{224... | collective-permute-start | bytes 147464 | tf_op jit(solution)/shard_map/ppermute | solution.py:202
  130.6 1.2 collective-permute-done.6.moved_ref
  131.7 0.4 shard_map.102
  132.1 13.3 %all_to_all.46 = bf16[16,8,3072]{2,1,0:T(8,128)(2,1)S(1)} all-to-all(bf16[16,8,3072]{2,1,0:T(8,128)(2,1)S(1)} %get-tuple-element.27), channel_id=1, replica_groups={{0,8,16,24,2,10,18,26,4,12,20,28,6,14,22,30},{1,3,5,7,9,11,13,15,17,19,..., dimensions={0} | all-to-all | bytes 1572864 | tf_op jit(solution)/shard_map/all_to_all | solution.py:168
  145.5 1.8 %shard_map.103 = bf16[128,3072]{1,0:T(8,128)(2,1)S(1)} custom-call(bf16[128,3072]{1,0:T(8,128)(2,1)S(1)} %bitcast.9, bf16[1,6144,128]{2,1,0:T(8,128)(2,1)S(1)} %copy-done, bf16[1,6144,128]{2,1,0:T(8,128)(2,1)S(1)} %collective-permute-done.2.up_far, bf16[1,128]{1,0:T(2,128)(2,1)S(1)} %copy-done.9, bf16[1,128]{1,0:T(2,128)(2,1)S(1)} %collective-permute-done.1.bias_far, ...), custom_call_target="tpu_custom_call" | custom-call | tf_op jit(solution)/shard_map/pallas_call | solution.py:141
  147.3 13.3 %all_to_all.47.parts_ref = bf16[16,8,3072]{2,1,0:T(8,128)(2,1)S(1)} all-to-all(bf16[16,8,3072]{2,1,0:T(8,128)(2,1)S(1)} %bitcast.10), channel_id=1, replica_groups={{0,8,16,24,2,10,18,26,4,12,20,28,6,14,22,30},{1,3,5,7,9,11,13,15,17,19,..., dimensions={0} | all-to-all | bytes 1572864 | tf_op jit(solution)/shard_map/all_to_all | solution.py:168
  160.6 0.1 shard_map.104
  160.7 12.5 %collective-permute-start.7 = (bf16[4,8,3072]{2,1,0:T(8,128)(2,1)S(1)}, bf16[4,8,3072]{2,1,0:T(8,128)(2,1)S(1)}, u32[]{:S(2)}, u32[]{:S(2)}) collective-permute-start(bf16[4,8,3072]{2,1,0:T(8,128)(2,1)S(1)} %shard_map.104), channel_id=1, source_target_pairs={{0,0},{24,1},{2,2},{26,3},{4,4},{28,5},{6,6},{30,7},{8,8},{16,9},{... | collective-permute-start | bytes 589832 | tf_op jit(solution)/shard_map/ppermute | solution.py:205
  173.2 3.3 %collective-permute-done.7.rows_ref = bf16[4,8,3072]{2,1,0:T(8,128)(2,1)S(1)} collective-permute-done((bf16[4,8,3072]{2,1,0:T(8,128)(2,1)S(1)}, bf16[4,8,3072]{2,1,0:T(8,128)(2,1)S(1)}, u32[]{:S(2)}, u32[]{:S(2)}) %collective-permute-start.7) | collective-permute-done | bytes 196640 | tf_op jit(solution)/shard_map/ppermute | solution.py:205
  176.6 0.7 shard_map.105
  (11 shorter events, 0.1 us)
Async XLA Ops:
  0.0 37.9 %copy-start = (bf16[1,6144,128]{2,1,0:T(8,128)(2,1)S(1)}, bf16[1,6144,128]{2,1,0:T(8,128)(2,1)}, u32[]{:S(2)}) copy-start(bf16[1,6144,128]{2,1,0:T(8,128)(2,1)} %up_near.7) | copy-start | bytes 4718596
  0.0 37.9 %collective-permute-start.2 = (bf16[1,6144,128]{2,1,0:T(8,128)(2,1)}, bf16[1,6144,128]{2,1,0:T(8,128)(2,1)S(1)}, u32[]{:S(2)}, u32[]{:S(2)}) collective-permute-start(bf16[1,6144,128]{2,1,0:T(8,128)(2,1)} %up_near.7), channel_id=1, source_target_pairs={{0,1},{1,0},{2,3},{3,2},{4,5},{5,4},{6,7},{7,6},{8,9},{9,8},{10,11... | collective-permute-start | bytes 4718600 | tf_op jit(solution)/shard_map/ppermute | solution.py:165
  8.9 29.0 %collective-permute-start.3 = (bf16[1,128,6144]{2,1,0:T(8,128)(2,1)}, bf16[1,128,6144]{2,1,0:T(8,128)(2,1)S(1)}, u32[]{:S(2)}, u32[]{:S(2)}) collective-permute-start(bf16[1,128,6144]{2,1,0:T(8,128)(2,1)} %down_near.7), channel_id=1, source_target_pairs={{0,1},{1,0},{2,3},{3,2},{4,5},{5,4},{6,7},{7,6},{8,9},{9,8},{10,11... | collective-permute-start | bytes 4718600 | tf_op jit(solution)/shard_map/ppermute | solution.py:165
  10.8 0.9 copy-start.4
  11.8 0.8 copy-start.6
  12.6 25.4 %copy-start.5 = (s32[4,1,2,16]{3,2,1,0:T(2,128)S(1)}, s32[4,1,2,16]{3,2,1,0:T(2,128)}, u32[]{:S(2)}) copy-start(s32[4,1,2,16]{3,2,1,0:T(2,128)} %active_ref.7) | copy-start | bytes 1540
  12.7 8.2 %collective-permute-start = (bf16[4,8,3072]{2,1,0:T(8,128)(2,1)S(1)}, bf16[4,8,3072]{2,1,0:T(8,128)(2,1)S(1)}, u32[]{:S(2)}, u32[]{:S(2)}) collective-permute-start(bf16[4,8,3072]{2,1,0:T(8,128)(2,1)S(1)} %shard_map.91), channel_id=1, source_target_pairs={{0,0},{1,24},{2,2},{3,26},{4,4},{5,28},{6,6},{7,30},{8,8},{9,16},{... | collective-permute-start | bytes 589832 | tf_op jit(solution)/shard_map/ppermute | solution.py:177
  14.6 3.5 %collective-permute-start.1 = (bf16[1,128]{1,0:T(2,128)(2,1)}, bf16[1,128]{1,0:T(2,128)(2,1)S(1)}, u32[]{:S(2)}, u32[]{:S(2)}) collective-permute-start(bf16[1,128]{1,0:T(2,128)(2,1)} %bias_near.7), channel_id=1, source_target_pairs={{0,1},{1,0},{2,3},{3,2},{4,5},{5,4},{6,7},{7,6},{8,9},{9,8},{10,11... | collective-permute-start | bytes 776 | tf_op jit(solution)/shard_map/ppermute | solution.py:165
  16.5 0.7 copy-start.7
  17.3 0.7 copy-start.8
  18.0 19.9 %copy-start.9 = (bf16[1,128]{1,0:T(2,128)(2,1)S(1)}, bf16[1,128]{1,0:T(2,128)(2,1)}, u32[]{:S(2)}) copy-start(bf16[1,128]{1,0:T(2,128)(2,1)} %bias_near.7) | copy-start | bytes 772
  37.9 1.4 copy-start.1
  41.1 16.4 %copy-start.3 = (bf16[1,6144]{1,0:T(2,128)(2,1)S(1)}, bf16[1,6144]{1,0:T(2,128)(2,1)}, u32[]{:S(2)}) copy-start(bf16[1,6144]{1,0:T(2,128)(2,1)} %bias_ref.7) | copy-start | bytes 36868
  57.5 19.2 %copy-start.2 = (bf16[1,128,6144]{2,1,0:T(8,128)(2,1)S(1)}, bf16[1,128,6144]{2,1,0:T(8,128)(2,1)}, u32[]{:S(2)}) copy-start(bf16[1,128,6144]{2,1,0:T(8,128)(2,1)} %down_near.7) | copy-start | bytes 4718596
  57.7 2.6 %collective-permute-start.4 = (bf16[8,3072]{1,0:T(8,128)(2,1)S(1)}, bf16[8,3072]{1,0:T(8,128)(2,1)S(1)}, u32[]{:S(2)}, u32[]{:S(2)}) collective-permute-start(bf16[8,3072]{1,0:T(8,128)(2,1)S(1)} %shard_map.95.refs_0_), channel_id=1, source_target_pairs={{0,32},{32,64},{64,96},{96,128},{128,160},{160,192},{192,224},{224... | collective-permute-start | bytes 147464 | tf_op jit(solution)/shard_map/ppermute | solution.py:202
  94.4 3.4 %collective-permute-start.5 = (bf16[8,3072]{1,0:T(8,128)(2,1)S(1)}, bf16[8,3072]{1,0:T(8,128)(2,1)S(1)}, u32[]{:S(2)}, u32[]{:S(2)}) collective-permute-start(bf16[8,3072]{1,0:T(8,128)(2,1)S(1)} %shard_map.98.refs_1_), channel_id=1, source_target_pairs={{0,32},{32,64},{64,96},{96,128},{128,160},{160,192},{192,224},{224... | collective-permute-start | bytes 147464 | tf_op jit(solution)/shard_map/ppermute | solution.py:202
  126.9 4.8 %collective-permute-start.6 = (bf16[8,3072]{1,0:T(8,128)(2,1)S(1)}, bf16[8,3072]{1,0:T(8,128)(2,1)S(1)}, u32[]{:S(2)}, u32[]{:S(2)}) collective-permute-start(bf16[8,3072]{1,0:T(8,128)(2,1)S(1)} %shard_map.101.refs_2_), channel_id=1, source_target_pairs={{0,32},{32,64},{64,96},{96,128},{128,160},{160,192},{192,224},{224... | collective-permute-start | bytes 147464 | tf_op jit(solution)/shard_map/ppermute | solution.py:202
  160.7 15.9 %collective-permute-start.7 = (bf16[4,8,3072]{2,1,0:T(8,128)(2,1)S(1)}, bf16[4,8,3072]{2,1,0:T(8,128)(2,1)S(1)}, u32[]{:S(2)}, u32[]{:S(2)}) collective-permute-start(bf16[4,8,3072]{2,1,0:T(8,128)(2,1)S(1)} %shard_map.104), channel_id=1, source_target_pairs={{0,0},{24,1},{2,2},{26,3},{4,4},{28,5},{6,6},{30,7},{8,8},{16,9},{... | collective-permute-start | bytes 589832 | tf_op jit(solution)/shard_map/ppermute | solution.py:205

commit v5 on v4

--- a/solution.py
+++ b/solution.py
@@ -15,7 +15,7 @@
 VMEM = pl.BlockSpec(memory_space=pltpu.VMEM)
 SMEM = pl.BlockSpec(memory_space=pltpu.SMEM)
 COST = pl.CostEstimate(flops=100_000, bytes_accessed=300_000, transcendentals=0)
-PARAMS = pltpu.CompilerParams(vmem_limit_bytes=40 * 1024 * 1024)
+PARAMS = pltpu.CompilerParams(vmem_limit_bytes=16 * 1024 * 1024)
 
 
 def is_first(shape):
@@ -66,10 +66,11 @@
         send_out[chip] = normed
 
 
-def ffn_kernel(step, rows_ref, up_near, up_far, bias_near, bias_far, active_ref, down_near, down_far, out_ref):
+def ffn_kernel(step, rows_ref, up_near, up_far, bias_near, active_ref, down_near, down_far, out_ref):
     count, half = rows_ref.shape
     block = up_near.shape[2]
-    chunk = 512
+    bias_far = up_far[0, 2 * half : 2 * half + 16, :].astype(F32)[:1]
+    chunk = 1024
     j = lax.axis_index("blk")
     tile = j % 2
 
@@ -95,7 +96,7 @@
             found = found | (active_ref[step, 0, tile, k] == owner).astype(jnp.int32)
         flags.append(jnp.broadcast_to(found.astype(F32), (1, block)))
     flag = jnp.concatenate(flags, axis=1)
-    bias = jnp.concatenate([bias_near[...], bias_far[...]], axis=1).astype(F32)
+    bias = jnp.concatenate([bias_near[...].astype(F32), bias_far], axis=1)
     acts = (jnp.maximum(preact + bias, 0.0) * flag).astype(BF16)
     low = is_first((count, chunk))
     for at in range(0, half, chunk):
@@ -167,7 +168,8 @@
     def trade(x):
         return lax.all_to_all(x, "blk", 0, 0, axis_index_groups=same_core, tiled=True)
 
-    up_far, down_far = swap(up_weight), swap(down_weight)
+    below = jnp.pad(up_bias[:, None], ((0, 0), (0, 15), (0, 0)))
+    up_far, down_far = swap(jnp.concatenate([up_weight, below], axis=1)), swap(down_weight)
     arranged = call(
         arrange_kernel,
         shape((TICKS, rows_half, half), BF16),
@@ -176,8 +178,6 @@
     )
     local = lax.ppermute(arranged, "blk", go_home)
     gain, bias = call(halves_kernel, [shape((rows_half, half), F32)] * 2, ln_gain, ln_bias, cost=COST)
-    bias_far = swap(up_bias)
-    local, bias_far = lax.optimization_barrier((local, bias_far))
     moved = None
     produced = []
     for step in range(TICKS):
@@ -192,8 +192,8 @@
         partial = call(
             functools.partial(ffn_kernel, step),
             shape((CHIPS * rows_half, half), BF16),
-            gathered, up_weight, up_far, up_bias, bias_far, active, down_weight, down_far,
-            specs=[VMEM] * 5 + [SMEM] + [VMEM] * 2,
+            gathered, up_weight, up_far, up_bias, active, down_weight, down_far,
+            specs=[VMEM] * 4 + [SMEM] + [VMEM] * 2,
         )
         received = trade(partial.reshape(CHIPS, rows_half, half))
         if step + 1 < TICKS:

time: 178 us -> 176 us (0.989)
  local copies, waits for them, and re-layouts: 4.59 us -> 0.04 us
  waiting for transfers between devices: 9.62 us -> 13 us
  starting transfers between devices: 34.5 us -> 32.5 us
    unnamed x20 -> x18, local copies, waits for them, and re-layouts: 4.59 us -> 0.04 us
    ppermute x1, waiting for transfers between devices: 2.8 us -> 6.2 us  [on_device(): local = lax.ppermute(arranged, 'blk', go_home)]
    ppermute x3 -> x2, starting transfers between devices: 12.8 us -> 10.8 us  [swap(): return lax.ppermute(x, 'blk', [(i, i ^ 1) for i in range(blocks)])]
  transfers between devices with their start and end apart: 8 -> 7, of which waited for: 5 -> 5; matrix products, arithmetic and copies ran while one was open for 0% -> 0% of each run, Pallas kernels for 0% -> 0%
where the time goes in v5:
time: 176 us
  blocking collectives  118 us (67%)
  starting transfers between devices  32.5 us (18%)
  waiting for transfers between devices  13 us (7%)
  Pallas kernels  10.1 us (6%)
    all_to_all x8, blocking collectives, trade(): lax.all_to_all(x, 'blk', 0, 0, axis_index_groups=same_core, tiled=True)  118 us
    ppermute x1, starting transfers between devices, on_device(): lax.ppermute(done, 'blk', [(home, j) for j, home in enumerate(homes)])  12.5 us
    ppermute x2, starting transfers between devices, swap(): return lax.ppermute(x, 'blk', [(i, i ^ 1) for i in range(blocks)])  10.8 us
    pallas_call x15, Pallas kernels, call(): pl.pallas_call(kernel, out_shape=outs, in_specs=list(specs) if specs else...  10.1 us
    ppermute x3, starting transfers between devices, on_device(): moved = lax.ppermute(done, 'pipe', [(i, i + 1) for i in range(pipes - 1)])  7.24 us
    ppermute x1, waiting for transfers between devices, on_device(): local = lax.ppermute(arranged, 'blk', go_home)  6.2 us
  transfers between devices with their start and end apart: 7, of which 5 were waited for; matrix products, arithmetic and copies ran while one was open for 0% of the time, Pallas kernels for 0%

profile of v5, /device:TPU:1, one launch (start us, length us, event | category | flops | bytes accessed | tf_op | source)
XLA Modules:
  0.0 175.7 jit_solution(894976598177183855)
XLA Ops:
  0.0 0.0 copy-start.6
  0.0 0.0 copy-start.7
  0.0 1.7 fusion.1
  1.7 0.0 copy-start
  1.7 0.0 copy-start.4
  1.7 0.0 copy-start.8
  1.7 8.9 %collective-permute-start.1 = (bf16[1,6160,128]{2,1,0:T(8,128)(2,1)S(1)}, bf16[1,6160,128]{2,1,0:T(8,128)(2,1)S(1)}, u32[]{:S(2)}, u32[]{:S(2)}) collective-permute-start(bf16[1,6160,128]{2,1,0:T(8,128)(2,1)S(1)} %fusion.1), channel_id=1, source_target_pairs={{0,1},{1,0},{2,3},{3,2},{4,5},{5,4},{6,7},{7,6},{8,9},{9,8},{10,11... | collective-permute-start | bytes 4730888 | tf_op jit(solution)/shard_map/ppermute | solution.py:166
  10.6 0.0 copy-done.1
  10.6 1.9 %collective-permute-start.2 = (bf16[1,128,6144]{2,1,0:T(8,128)(2,1)S(1)}, bf16[1,128,6144]{2,1,0:T(8,128)(2,1)S(1)}, u32[]{:S(2)}, u32[]{:S(2)}) collective-permute-start(bf16[1,128,6144]{2,1,0:T(8,128)(2,1)S(1)} %copy-done.1), channel_id=1, source_target_pairs={{0,1},{1,0},{2,3},{3,2},{4,5},{5,4},{6,7},{7,6},{8,9},{9,8},{10,11... | collective-permute-start | bytes 4718600 | tf_op jit(solution)/shard_map/ppermute | solution.py:166
  12.6 0.1 shard_map.91
  12.7 1.9 %collective-permute-start = (bf16[4,8,3072]{2,1,0:T(8,128)(2,1)S(1)}, bf16[4,8,3072]{2,1,0:T(8,128)(2,1)S(1)}, u32[]{:S(2)}, u32[]{:S(2)}) collective-permute-start(bf16[4,8,3072]{2,1,0:T(8,128)(2,1)S(1)} %shard_map.91), channel_id=1, source_target_pairs={{0,0},{1,24},{2,2},{3,26},{4,4},{5,28},{6,6},{7,30},{8,8},{9,16},{... | collective-permute-start | bytes 589832 | tf_op jit(solution)/shard_map/ppermute | solution.py:179
  14.6 0.0 copy-done.6
  14.6 0.0 copy-done.7
  14.7 6.2 %collective-permute-done.local_ref = bf16[4,8,3072]{2,1,0:T(8,128)(2,1)S(1)} collective-permute-done((bf16[4,8,3072]{2,1,0:T(8,128)(2,1)S(1)}, bf16[4,8,3072]{2,1,0:T(8,128)(2,1)S(1)}, u32[]{:S(2)}, u32[]{:S(2)}) %collective-permute-start) | collective-permute-done | bytes 196640 | tf_op jit(solution)/shard_map/ppermute | solution.py:179
  20.9 0.4 shard_map.93
  21.3 16.7 %all_to_all.40 = bf16[16,8,3072]{2,1,0:T(8,128)(2,1)S(1)} all-to-all(bf16[16,8,3072]{2,1,0:T(8,128)(2,1)S(1)} %get-tuple-element.17), channel_id=1, replica_groups={{0,8,16,24,2,10,18,26,4,12,20,28,6,14,22,30},{1,3,5,7,9,11,13,15,17,19,..., dimensions={0} | all-to-all | bytes 1572864 | tf_op jit(solution)/shard_map/all_to_all | solution.py:169
  38.0 0.0 collective-permute-done.2.down_far
  38.0 0.0 collective-permute-done.1.up_far
  38.0 0.0 copy-done.4
  38.0 0.0 copy-done.8
  38.0 1.8 %shard_map.94 = bf16[128,3072]{1,0:T(8,128)(2,1)S(1)} custom-call(bf16[128,3072]{1,0:T(8,128)(2,1)S(1)} %bitcast.9, bf16[1,6144,128]{2,1,0:T(8,128)(2,1)S(1)} %copy-done, bf16[1,6160,128]{2,1,0:T(8,128)(2,1)S(1)} %collective-permute-done.1.up_far, bf16[1,128]{1,0:T(2,128)(2,1)S(1)} %copy-done.8, s32[4,1,2,16]{3,2,1,0:T(2,128)S(1)} %copy-done.4, ...), custom_call_target="tpu_custom_call" | custom-call | tf_op jit(solution)/shard_map/pallas_call | solution.py:142
  39.8 0.0 copy-start.2
  39.8 16.3 %all_to_all.41.parts_ref = bf16[16,8,3072]{2,1,0:T(8,128)(2,1)S(1)} all-to-all(bf16[16,8,3072]{2,1,0:T(8,128)(2,1)S(1)} %bitcast.12), channel_id=1, replica_groups={{0,8,16,24,2,10,18,26,4,12,20,28,6,14,22,30},{1,3,5,7,9,11,13,15,17,19,..., dimensions={0} | all-to-all | bytes 1572864 | tf_op jit(solution)/shard_map/all_to_all | solution.py:169
  56.1 0.1 shard_map.95.refs_0_
  56.3 1.3 collective-permute-start.3
  57.6 1.2 collective-permute-done.3.moved_ref
  58.7 0.4 shard_map.96
  59.1 16.0 %all_to_all.42 = bf16[16,8,3072]{2,1,0:T(8,128)(2,1)S(1)} all-to-all(bf16[16,8,3072]{2,1,0:T(8,128)(2,1)S(1)} %get-tuple-element.19), channel_id=1, replica_groups={{0,8,16,24,2,10,18,26,4,12,20,28,6,14,22,30},{1,3,5,7,9,11,13,15,17,19,..., dimensions={0} | all-to-all | bytes 1572864 | tf_op jit(solution)/shard_map/all_to_all | solution.py:169
  75.2 1.8 %shard_map.97 = bf16[128,3072]{1,0:T(8,128)(2,1)S(1)} custom-call(bf16[128,3072]{1,0:T(8,128)(2,1)S(1)} %bitcast.13, bf16[1,6144,128]{2,1,0:T(8,128)(2,1)S(1)} %copy-done, bf16[1,6160,128]{2,1,0:T(8,128)(2,1)S(1)} %collective-permute-done.1.up_far, bf16[1,128]{1,0:T(2,128)(2,1)S(1)} %copy-done.8, s32[4,1,2,16]{3,2,1,0:T(2,128)S(1)} %copy-done.4, ...), custom_call_target="tpu_custom_call" | custom-call | tf_op jit(solution)/shard_map/pallas_call | solution.py:142
  76.9 15.7 %all_to_all.43.parts_ref = bf16[16,8,3072]{2,1,0:T(8,128)(2,1)S(1)} all-to-all(bf16[16,8,3072]{2,1,0:T(8,128)(2,1)S(1)} %bitcast.14), channel_id=1, replica_groups={{0,8,16,24,2,10,18,26,4,12,20,28,6,14,22,30},{1,3,5,7,9,11,13,15,17,19,..., dimensions={0} | all-to-all | bytes 1572864 | tf_op jit(solution)/shard_map/all_to_all | solution.py:169
  92.7 0.1 shard_map.98.refs_1_
  92.8 2.3 %collective-permute-start.4 = (bf16[8,3072]{1,0:T(8,128)(2,1)S(1)}, bf16[8,3072]{1,0:T(8,128)(2,1)S(1)}, u32[]{:S(2)}, u32[]{:S(2)}) collective-permute-start(bf16[8,3072]{1,0:T(8,128)(2,1)S(1)} %shard_map.98.refs_1_), channel_id=1, source_target_pairs={{0,32},{32,64},{64,96},{96,128},{128,160},{160,192},{192,224},{224... | collective-permute-start | bytes 147464 | tf_op jit(solution)/shard_map/ppermute | solution.py:202
  95.1 1.2 collective-permute-done.4.moved_ref
  96.3 0.4 shard_map.99
  96.7 13.1 %all_to_all.44 = bf16[16,8,3072]{2,1,0:T(8,128)(2,1)S(1)} all-to-all(bf16[16,8,3072]{2,1,0:T(8,128)(2,1)S(1)} %get-tuple-element.21), channel_id=1, replica_groups={{0,8,16,24,2,10,18,26,4,12,20,28,6,14,22,30},{1,3,5,7,9,11,13,15,17,19,..., dimensions={0} | all-to-all | bytes 1572864 | tf_op jit(solution)/shard_map/all_to_all | solution.py:169
  109.8 1.8 %shard_map.100 = bf16[128,3072]{1,0:T(8,128)(2,1)S(1)} custom-call(bf16[128,3072]{1,0:T(8,128)(2,1)S(1)} %bitcast.15, bf16[1,6144,128]{2,1,0:T(8,128)(2,1)S(1)} %copy-done, bf16[1,6160,128]{2,1,0:T(8,128)(2,1)S(1)} %collective-permute-done.1.up_far, bf16[1,128]{1,0:T(2,128)(2,1)S(1)} %copy-done.8, s32[4,1,2,16]{3,2,1,0:T(2,128)S(1)} %copy-done.4, ...), custom_call_target="tpu_custom_call" | custom-call | tf_op jit(solution)/shard_map/pallas_call | solution.py:142
  111.5 13.6 %all_to_all.45.parts_ref = bf16[16,8,3072]{2,1,0:T(8,128)(2,1)S(1)} all-to-all(bf16[16,8,3072]{2,1,0:T(8,128)(2,1)S(1)} %bitcast.16), channel_id=1, replica_groups={{0,8,16,24,2,10,18,26,4,12,20,28,6,14,22,30},{1,3,5,7,9,11,13,15,17,19,..., dimensions={0} | all-to-all | bytes 1572864 | tf_op jit(solution)/shard_map/all_to_all | solution.py:169
  125.1 0.1 shard_map.101.refs_2_
  125.3 3.7 %collective-permute-start.5 = (bf16[8,3072]{1,0:T(8,128)(2,1)S(1)}, bf16[8,3072]{1,0:T(8,128)(2,1)S(1)}, u32[]{:S(2)}, u32[]{:S(2)}) collective-permute-start(bf16[8,3072]{1,0:T(8,128)(2,1)S(1)} %shard_map.101.refs_2_), channel_id=1, source_target_pairs={{0,32},{32,64},{64,96},{96,128},{128,160},{160,192},{192,224},{224... | collective-permute-start | bytes 147464 | tf_op jit(solution)/shard_map/ppermute | solution.py:202
  129.0 1.2 collective-permute-done.5.moved_ref
  130.1 0.4 shard_map.102
  130.5 13.3 %all_to_all.46 = bf16[16,8,3072]{2,1,0:T(8,128)(2,1)S(1)} all-to-all(bf16[16,8,3072]{2,1,0:T(8,128)(2,1)S(1)} %get-tuple-element.23), channel_id=1, replica_groups={{0,8,16,24,2,10,18,26,4,12,20,28,6,14,22,30},{1,3,5,7,9,11,13,15,17,19,..., dimensions={0} | all-to-all | bytes 1572864 | tf_op jit(solution)/shard_map/all_to_all | solution.py:169
  143.9 1.8 %shard_map.103 = bf16[128,3072]{1,0:T(8,128)(2,1)S(1)} custom-call(bf16[128,3072]{1,0:T(8,128)(2,1)S(1)} %bitcast.10, bf16[1,6144,128]{2,1,0:T(8,128)(2,1)S(1)} %copy-done, bf16[1,6160,128]{2,1,0:T(8,128)(2,1)S(1)} %collective-permute-done.1.up_far, bf16[1,128]{1,0:T(2,128)(2,1)S(1)} %copy-done.8, s32[4,1,2,16]{3,2,1,0:T(2,128)S(1)} %copy-done.4, ...), custom_call_target="tpu_custom_call" | custom-call | tf_op jit(solution)/shard_map/pallas_call | solution.py:142
  145.6 13.3 %all_to_all.47.parts_ref = bf16[16,8,3072]{2,1,0:T(8,128)(2,1)S(1)} all-to-all(bf16[16,8,3072]{2,1,0:T(8,128)(2,1)S(1)} %bitcast.11), channel_id=1, replica_groups={{0,8,16,24,2,10,18,26,4,12,20,28,6,14,22,30},{1,3,5,7,9,11,13,15,17,19,..., dimensions={0} | all-to-all | bytes 1572864 | tf_op jit(solution)/shard_map/all_to_all | solution.py:169
  159.0 0.1 shard_map.104
  159.1 12.5 %collective-permute-start.6 = (bf16[4,8,3072]{2,1,0:T(8,128)(2,1)S(1)}, bf16[4,8,3072]{2,1,0:T(8,128)(2,1)S(1)}, u32[]{:S(2)}, u32[]{:S(2)}) collective-permute-start(bf16[4,8,3072]{2,1,0:T(8,128)(2,1)S(1)} %shard_map.104), channel_id=1, source_target_pairs={{0,0},{24,1},{2,2},{26,3},{4,4},{28,5},{6,6},{30,7},{8,8},{16,9},{... | collective-permute-start | bytes 589832 | tf_op jit(solution)/shard_map/ppermute | solution.py:205
  171.6 3.3 %collective-permute-done.6.rows_ref = bf16[4,8,3072]{2,1,0:T(8,128)(2,1)S(1)} collective-permute-done((bf16[4,8,3072]{2,1,0:T(8,128)(2,1)S(1)}, bf16[4,8,3072]{2,1,0:T(8,128)(2,1)S(1)}, u32[]{:S(2)}, u32[]{:S(2)}) %collective-permute-start.6) | collective-permute-done | bytes 196640 | tf_op jit(solution)/shard_map/ppermute | solution.py:205
  175.0 0.7 shard_map.105
  (8 shorter events, 0.1 us)
Async XLA Ops:
  0.0 10.6 %copy-start.1 = (bf16[1,128,6144]{2,1,0:T(8,128)(2,1)S(1)}, bf16[1,128,6144]{2,1,0:T(8,128)(2,1)}, u32[]{:S(2)}) copy-start(bf16[1,128,6144]{2,1,0:T(8,128)(2,1)} %down_near.7) | copy-start | bytes 4718596
  0.0 12.6 %copy-start.3 = (bf16[3,4,6144]{2,1,0:T(4,128)(2,1)S(1)}, bf16[3,4,6144]{2,1,0:T(4,128)(2,1)}, u32[]{:S(2)}) copy-start(bf16[3,4,6144]{2,1,0:T(4,128)(2,1)} %arrivals_ref.1) | copy-start | bytes 442372
  0.0 12.6 %copy-start.5 = (bf16[1,4,6144]{2,1,0:T(4,128)(2,1)S(1)}, bf16[1,4,6144]{2,1,0:T(4,128)(2,1)}, u32[]{:S(2)}) copy-start(bf16[1,4,6144]{2,1,0:T(4,128)(2,1)} %stream_ref.1) | copy-start | bytes 147460
  0.0 14.6 %copy-start.6 = (bf16[1,6144]{1,0:T(2,128)(2,1)S(1)}, bf16[1,6144]{1,0:T(2,128)(2,1)}, u32[]{:S(2)}) copy-start(bf16[1,6144]{1,0:T(2,128)(2,1)} %gain.1) | copy-start | bytes 36868
  0.0 14.6 %copy-start.7 = (bf16[1,6144]{1,0:T(2,128)(2,1)S(1)}, bf16[1,6144]{1,0:T(2,128)(2,1)}, u32[]{:S(2)}) copy-start(bf16[1,6144]{1,0:T(2,128)(2,1)} %bias.1) | copy-start | bytes 36868
  1.7 36.3 %copy-start = (bf16[1,6144,128]{2,1,0:T(8,128)(2,1)S(1)}, bf16[1,6144,128]{2,1,0:T(8,128)(2,1)}, u32[]{:S(2)}) copy-start(bf16[1,6144,128]{2,1,0:T(8,128)(2,1)} %up_near.7) | copy-start | bytes 4718596
  1.7 36.3 %copy-start.4 = (s32[4,1,2,16]{3,2,1,0:T(2,128)S(1)}, s32[4,1,2,16]{3,2,1,0:T(2,128)}, u32[]{:S(2)}) copy-start(s32[4,1,2,16]{3,2,1,0:T(2,128)} %active_ref.7) | copy-start | bytes 1540
  1.7 36.3 %copy-start.8 = (bf16[1,128]{1,0:T(2,128)(2,1)S(1)}, bf16[1,128]{1,0:T(2,128)(2,1)}, u32[]{:S(2)}) copy-start(bf16[1,128]{1,0:T(2,128)(2,1)} %bias_near.7) | copy-start | bytes 772
  1.7 36.2 %collective-permute-start.1 = (bf16[1,6160,128]{2,1,0:T(8,128)(2,1)S(1)}, bf16[1,6160,128]{2,1,0:T(8,128)(2,1)S(1)}, u32[]{:S(2)}, u32[]{:S(2)}) collective-permute-start(bf16[1,6160,128]{2,1,0:T(8,128)(2,1)S(1)} %fusion.1), channel_id=1, source_target_pairs={{0,1},{1,0},{2,3},{3,2},{4,5},{5,4},{6,7},{7,6},{8,9},{9,8},{10,11... | collective-permute-start | bytes 4730888 | tf_op jit(solution)/shard_map/ppermute | solution.py:166
  10.6 27.3 %collective-permute-start.2 = (bf16[1,128,6144]{2,1,0:T(8,128)(2,1)S(1)}, bf16[1,128,6144]{2,1,0:T(8,128)(2,1)S(1)}, u32[]{:S(2)}, u32[]{:S(2)}) collective-permute-start(bf16[1,128,6144]{2,1,0:T(8,128)(2,1)S(1)} %copy-done.1), channel_id=1, source_target_pairs={{0,1},{1,0},{2,3},{3,2},{4,5},{5,4},{6,7},{7,6},{8,9},{9,8},{10,11... | collective-permute-start | bytes 4718600 | tf_op jit(solution)/shard_map/ppermute | solution.py:166
  12.7 8.2 %collective-permute-start = (bf16[4,8,3072]{2,1,0:T(8,128)(2,1)S(1)}, bf16[4,8,3072]{2,1,0:T(8,128)(2,1)S(1)}, u32[]{:S(2)}, u32[]{:S(2)}) collective-permute-start(bf16[4,8,3072]{2,1,0:T(8,128)(2,1)S(1)} %shard_map.91), channel_id=1, source_target_pairs={{0,0},{1,24},{2,2},{3,26},{4,4},{5,28},{6,6},{7,30},{8,8},{9,16},{... | collective-permute-start | bytes 589832 | tf_op jit(solution)/shard_map/ppermute | solution.py:179
  39.8 16.4 %copy-start.2 = (bf16[1,6144]{1,0:T(2,128)(2,1)S(1)}, bf16[1,6144]{1,0:T(2,128)(2,1)}, u32[]{:S(2)}) copy-start(bf16[1,6144]{1,0:T(2,128)(2,1)} %bias_ref.7) | copy-start | bytes 36868
  56.3 2.5 %collective-permute-start.3 = (bf16[8,3072]{1,0:T(8,128)(2,1)S(1)}, bf16[8,3072]{1,0:T(8,128)(2,1)S(1)}, u32[]{:S(2)}, u32[]{:S(2)}) collective-permute-start(bf16[8,3072]{1,0:T(8,128)(2,1)S(1)} %shard_map.95.refs_0_), channel_id=1, source_target_pairs={{0,32},{32,64},{64,96},{96,128},{128,160},{160,192},{192,224},{224... | collective-permute-start | bytes 147464 | tf_op jit(solution)/shard_map/ppermute | solution.py:202
  92.8 3.5 %collective-permute-start.4 = (bf16[8,3072]{1,0:T(8,128)(2,1)S(1)}, bf16[8,3072]{1,0:T(8,128)(2,1)S(1)}, u32[]{:S(2)}, u32[]{:S(2)}) collective-permute-start(bf16[8,3072]{1,0:T(8,128)(2,1)S(1)} %shard_map.98.refs_1_), channel_id=1, source_target_pairs={{0,32},{32,64},{64,96},{96,128},{128,160},{160,192},{192,224},{224... | collective-permute-start | bytes 147464 | tf_op jit(solution)/shard_map/ppermute | solution.py:202
  125.3 4.8 %collective-permute-start.5 = (bf16[8,3072]{1,0:T(8,128)(2,1)S(1)}, bf16[8,3072]{1,0:T(8,128)(2,1)S(1)}, u32[]{:S(2)}, u32[]{:S(2)}) collective-permute-start(bf16[8,3072]{1,0:T(8,128)(2,1)S(1)} %shard_map.101.refs_2_), channel_id=1, source_target_pairs={{0,32},{32,64},{64,96},{96,128},{128,160},{160,192},{192,224},{224... | collective-permute-start | bytes 147464 | tf_op jit(solution)/shard_map/ppermute | solution.py:202
  159.1 15.8 %collective-permute-start.6 = (bf16[4,8,3072]{2,1,0:T(8,128)(2,1)S(1)}, bf16[4,8,3072]{2,1,0:T(8,128)(2,1)S(1)}, u32[]{:S(2)}, u32[]{:S(2)}) collective-permute-start(bf16[4,8,3072]{2,1,0:T(8,128)(2,1)S(1)} %shard_map.104), channel_id=1, source_target_pairs={{0,0},{24,1},{2,2},{26,3},{4,4},{28,5},{6,6},{30,7},{8,8},{16,9},{... | collective-permute-start | bytes 589832 | tf_op jit(solution)/shard_map/ppermute | solution.py:205
